TPU v7x, 256 devices: a whole 4x4x8 slice. The times are simulated.
256 devices in a mesh: seq: 32 (over z, y_lo, core), dp: 8 (over x, y_hi).
Axes of the slice: x: 4, y: 4 (y_hi: 2, y_lo: 2; y = y_hi * 2 + y_lo), z: 8, core: 2. Of those that a mesh axis runs over, the one named last changes fastest.
Arguments:
- enc_query: bfloat16 [32768, 4096], P(('dp', 'seq')), parts along dimension 0, may hold values from -6 to 6
- enc_key: bfloat16 [32768, 4096], P(('dp', 'seq')), parts along dimension 0, may hold values from -6 to 6
- enc_value: bfloat16 [32768, 4096], P(('dp', 'seq')), parts along dimension 0, may hold values from -6 to 6
- dec_query: bfloat16 [8192, 4096], P(('dp', 'seq')), parts along dimension 0, may hold values from -6 to 6
- enc_length: int32 [8], P('dp'), parts along dimension 0, may hold values from 2048 to 4096
- tgt_length: int32 [8], P('dp'), parts along dimension 0, may hold values from 512 to 1024
Outputs:
- enc_mixed: bfloat16 [32768, 4096], P(('dp', 'seq')), parts along dimension 0
- cross_mixed: bfloat16 [8192, 4096], P(('dp', 'seq')), parts along dimension 0
There are 8 independent parts, one for each index of `dp`. A program takes and returns all parts, laid end to end along the dimension named above; each array names one. Nothing has to cross between parts.
All inputs are finite; a program needn't handle non-finite values.
Results may differ from a plain program's by a relative error of at most 0.0049.
Values may be sent and summed in bfloat16 or wider, within the bound.
No kernel may reach another device: no remote copies, remote signals or barrier semaphores. Data moves between devices by JAX's collectives and lax.ppermute only.
A program may use at most 128 MiB of HBM per device.

v0:
```python
import jax
import jax.numpy as jnp
from jax import lax
from jax.sharding import PartitionSpec as P

DH = 64


score_scale = 0.125


def attend_block(queries, key_mat, values, valid_len):
    row_total = queries.shape[0]
    col_width = queries.shape[1]
    head_count = col_width // DH
    key_rows = key_mat.shape[0]
    row_block = min(512, row_total)
    blocks_num = row_total // row_block
    key_heads = key_mat.reshape(key_rows, head_count, DH)
    value_heads = values.reshape(key_rows, head_count, DH)
    live_keys = jnp.arange(key_rows, dtype=jnp.int32) < valid_len

    def one_block(query_block):
        query_heads = query_block.reshape(row_block, head_count, DH)
        scores = (
            jnp.einsum("bhd,khd->hbk", query_heads, key_heads, preferred_element_type=jnp.float32)
            * score_scale
        )
        scores = jnp.where(live_keys[None, None, :], scores, -1e30)
        row_max = jnp.max(scores, axis=-1, keepdims=True)
        weights = jnp.exp(scores - row_max)
        weights = (weights / jnp.sum(weights, axis=-1, keepdims=True)).astype(jnp.bfloat16)
        mixed_out = jnp.einsum(
            "hbk,khd->bhd", weights, value_heads, preferred_element_type=jnp.float32
        )
        return mixed_out.astype(jnp.bfloat16).reshape(row_block, col_width)

    result = lax.map(one_block, queries.reshape(blocks_num, row_block, col_width))
    return result.reshape(row_total, col_width)


def on_device(enc_query, enc_key, enc_value, dec_query, enc_length, tgt_length):
    valid_len = enc_length[0]
    rows_local = dec_query.shape[0]
    head_query, head_keys, head_values = (
        lax.all_to_all(enc_query, "seq", split_axis=1, concat_axis=0, tiled=True),
        lax.all_to_all(enc_key, "seq", split_axis=1, concat_axis=0, tiled=True),
        lax.all_to_all(enc_value, "seq", split_axis=1, concat_axis=0, tiled=True),
    )
    heads_mixed = attend_block(head_query, head_keys, head_values, valid_len)
    enc_mixed = lax.all_to_all(heads_mixed, "seq", split_axis=0, concat_axis=1, tiled=True)
    target_heads = lax.all_to_all(dec_query, "seq", split_axis=1, concat_axis=0, tiled=True)
    crossed = attend_block(target_heads, head_keys, head_values, valid_len)
    returned = lax.all_to_all(crossed, "seq", split_axis=0, concat_axis=1, tiled=True)
    first_row = lax.axis_index("seq") * rows_local
    keep_rows = first_row + jnp.arange(rows_local, dtype=jnp.int32) < tgt_length[0]
    cross_mixed = jnp.where(keep_rows[:, None], returned, jnp.zeros_like(returned))
    return (enc_mixed, cross_mixed)


def solution(mesh):
    return jax.shard_map(
        on_device,
        mesh=mesh,
        in_specs=(
            P(("dp", "seq"), None),
            P(("dp", "seq"), None),
            P(("dp", "seq"), None),
            P(("dp", "seq"), None),
            P("dp"),
            P("dp"),
        ),
        out_specs=(P(("dp", "seq"), None), P(("dp", "seq"), None)),
        check_vma=False,
    )
```

profile of v0, /device:TPU:2, one launch (start us, length us, event | category | flops | bytes accessed | tf_op | source)
XLA Modules:
  0.0 371.3 jit_solution(7365579133056750982)
XLA Ops:
  0.6 2.3 copy.42
  3.0 9.9 %all-to-all-start.1 = ((bf16[128,32,128]{0,2,1:T(8,128)(2,1)}), bf16[128,32,128]{0,2,1:T(8,128)(2,1)S(1)}, u32[]{:S(2)}, u32[]{:S(2)}) async-start(bf16[128,32,128]{0,2,1:T(8,128)(2,1)} %bitcast.3), calls=%async_computation.1 | async-start | bytes 2097152 | tf_op jit(solution)/shard_map/all_to_all | solution.py:47
  12.8 2.3 copy.44
  15.1 26.9 %all-to-all-done.1 = bf16[128,32,128]{0,2,1:T(8,128)(2,1)S(1)} async-done(((bf16[128,32,128]{0,2,1:T(8,128)(2,1)}), bf16[128,32,128]{0,2,1:T(8,128)(2,1)S(1)}, u32[]{:S(2)}, u32[]{:S(2)}) %all-to-all-start.1) | async-done | bytes 1048608 | tf_op jit(solution)/shard_map/all_to_all | solution.py:47
  41.9 3.9 %all-to-all-start.2 = ((bf16[128,32,128]{0,2,1:T(8,128)(2,1)}), bf16[128,32,128]{0,2,1:T(8,128)(2,1)S(1)}, u32[]{:S(2)}, u32[]{:S(2)}) async-start(bf16[128,32,128]{0,2,1:T(8,128)(2,1)} %bitcast.5), calls=%async_computation.2 | async-start | bytes 2097152 | tf_op jit(solution)/shard_map/all_to_all | solution.py:48
  45.9 2.3 copy.40
  48.1 27.0 %all-to-all-done.2 = bf16[128,32,128]{0,2,1:T(8,128)(2,1)S(1)} async-done(((bf16[128,32,128]{0,2,1:T(8,128)(2,1)}), bf16[128,32,128]{0,2,1:T(8,128)(2,1)S(1)}, u32[]{:S(2)}, u32[]{:S(2)}) %all-to-all-start.2) | async-done | bytes 1048608 | tf_op jit(solution)/shard_map/all_to_all | solution.py:48
  75.1 3.9 %all-to-all-start = ((bf16[128,32,128]{0,2,1:T(8,128)(2,1)}), bf16[128,32,128]{0,2,1:T(8,128)(2,1)S(1)}, u32[]{:S(2)}, u32[]{:S(2)}) async-start(bf16[128,32,128]{0,2,1:T(8,128)(2,1)} %bitcast.74), calls=%async_computation | async-start | bytes 2097152 | tf_op jit(solution)/shard_map/all_to_all | solution.py:46
  79.0 0.8 copy_bitcast_fusion
  79.8 28.5 %all-to-all-done = bf16[128,32,128]{0,2,1:T(8,128)(2,1)S(1)} async-done(((bf16[128,32,128]{0,2,1:T(8,128)(2,1)}), bf16[128,32,128]{0,2,1:T(8,128)(2,1)S(1)}, u32[]{:S(2)}, u32[]{:S(2)}) %all-to-all-start) | async-done | bytes 1048608 | tf_op jit(solution)/shard_map/all_to_all | solution.py:46
  108.3 4.6 %all-to-all-start.4 = ((bf16[32,32,128]{2,0,1:T(8,128)(2,1)}), bf16[32,32,128]{2,0,1:T(8,128)(2,1)}, u32[]{:S(2)}, u32[]{:S(2)}) async-start(bf16[32,32,128]{2,0,1:T(8,128)(2,1)} %copy_bitcast_fusion), calls=%async_computation.4 | async-start | bytes 524288 | tf_op jit(solution)/shard_map/all_to_all | solution.py:52
  112.9 1.6 copy.43
  114.5 2.3 reshape.68
  117.5 1.3 reshape.69
  119.4 5.8 %all-to-all-done.4 = bf16[32,32,128]{2,0,1:T(8,128)(2,1)} async-done(((bf16[32,32,128]{2,0,1:T(8,128)(2,1)}), bf16[32,32,128]{2,0,1:T(8,128)(2,1)}, u32[]{:S(2)}, u32[]{:S(2)}) %all-to-all-start.4) | async-done | bytes 262176 | tf_op jit(solution)/shard_map/all_to_all | solution.py:52
  125.2 42.2 %while.23 = (s32[]{:T(128)}, bf16[2,512,128]{2,1,0:T(8,128)(2,1)}, bf16[2,512,128]{2,1,0:T(8,128)(2,1)}, bf16[4096,2,64]{0,2,1:T(8,128)(2,1)}, bf16[4096,2,64]{0,2,1:T(8,128)(2,1)}, /*index=5*/s32[]{:T(128)}, s32[]{:T(128)}) while((s32[]{:T(128)}, bf16[2,512,128]{2,1,0:T(8,128)(2,1)}, bf16[2,512,128]{2,1,0:T(8,128)(2,1)}, ...), condition=%wide.region_7.8_spmd.clone, body=%wide.region_4.7_spmd.clone.sunk | while | flops 1098981376 | bytes 43270316 | solution.py:38
  125.2 1.0 constant_dynamic-slice_fusion.5
  127.0 9.9 %fusion.58 = (f32[2,512]{1,0:T(2,128)S(1)}, f32[2,512,4096]{2,1,0:T(8,128)}) fusion(pred[4096]{0:T(1024)(128)(4,1)S(1)} %iota_compare_fusion.5, bf16[512,2,64]{0,2,1:T(8,128)(2,1)S(1)} %bitcast.76, bf16[4096,2,64]{0,2,1:T(8,128)(2,1)} %get-tuple-element.300), kind=kOutput, calls=%fused_computation.38.clone.1 | convolution fusion | flops 553652224 | bytes 17965056 | tf_op jit(solution)/shard_map/while/body/eval_jaxpr/sub | solution.py:31
  136.9 8.5 %fusion.59 = bf16[2,512,64]{1,2,0:T(8,128)(2,1)S(1)} fusion(bf16[4096,2,64]{0,2,1:T(8,128)(2,1)S(1)} %copy-done.1, f32[2,512,4096]{2,1,0:T(8,128)} %get-tuple-element.260, f32[2,512]{1,0:T(2,128)S(1)} %get-tuple-element.261), kind=kOutput, calls=%fused_computation.28.clone.1 | convolution fusion | flops 545325056 | bytes 17960960 | tf_op jit(solution)/shard_map/while/body/eval_jaxpr/hbk,khd->bhd/dot_general | solution.py:33
  146.3 1.0 constant_dynamic-slice_fusion.5
  148.1 9.9 %fusion.58 = (f32[2,512]{1,0:T(2,128)S(1)}, f32[2,512,4096]{2,1,0:T(8,128)}) fusion(pred[4096]{0:T(1024)(128)(4,1)S(1)} %iota_compare_fusion.5, bf16[512,2,64]{0,2,1:T(8,128)(2,1)S(1)} %bitcast.76, bf16[4096,2,64]{0,2,1:T(8,128)(2,1)} %get-tuple-element.300), kind=kOutput, calls=%fused_computation.38.clone.1 | convolution fusion | flops 553652224 | bytes 17965056 | tf_op jit(solution)/shard_map/while/body/eval_jaxpr/sub | solution.py:31
  158.0 8.5 %fusion.59 = bf16[2,512,64]{1,2,0:T(8,128)(2,1)S(1)} fusion(bf16[4096,2,64]{0,2,1:T(8,128)(2,1)S(1)} %copy-done.1, f32[2,512,4096]{2,1,0:T(8,128)} %get-tuple-element.260, f32[2,512]{1,0:T(2,128)S(1)} %get-tuple-element.261), kind=kOutput, calls=%fused_computation.28.clone.1 | convolution fusion | flops 545325056 | bytes 17960960 | tf_op jit(solution)/shard_map/while/body/eval_jaxpr/hbk,khd->bhd/dot_general | solution.py:33
  167.4 4.0 %all-to-all-start.5 = ((bf16[32,32,128]{2,1,0:T(8,128)(2,1)}), bf16[32,32,128]{2,1,0:T(8,128)(2,1)S(1)}, u32[]{:S(2)}, u32[]{:S(2)}) async-start(bf16[32,32,128]{2,1,0:T(8,128)(2,1)} %bitcast.82), calls=%async_computation.5 | async-start | bytes 524288 | tf_op jit(solution)/shard_map/all_to_all | solution.py:54
  171.5 160.6 %while.22 = (s32[]{:T(128)}, bf16[8,512,128]{2,1,0:T(8,128)(2,1)}, bf16[8,512,128]{2,1,0:T(8,128)(2,1)S(1)}, bf16[4096,2,64]{0,2,1:T(8,128)(2,1)}, bf16[4096,2,64]{0,2,1:T(8,128)(2,1)}, /*index=5*/s32[]{:T(128)}, s32[]{:T(128)}) while((s32[]{:T(128)}, bf16[8,512,128]{2,1,0:T(8,128)(2,1)}, bf16[8,512,128]{2,1,0:T(8,128)(2,1)S(1)}, ...), condition=%wide.region_3.4_spmd.clone, body=%wide.region_0.3_spmd.clone.sunk | while | flops 1098981376 | bytes 41173616 | solution.py:38
  171.7 0.7 iota_compare_fusion.4
  172.4 9.9 %fusion.53 = (f32[2,512]{1,0:T(2,128)S(1)}, f32[2,512,4096]{2,1,0:T(8,128)}) fusion(pred[4096]{0:T(1024)(128)(4,1)S(1)} %iota_compare_fusion.4, bf16[512,2,64]{0,2,1:T(8,128)(2,1)S(1)} %bitcast.77, bf16[4096,2,64]{0,2,1:T(8,128)(2,1)} %get-tuple-element.279), kind=kOutput, calls=%fused_computation.37.clone.1 | convolution fusion | flops 553652224 | bytes 17965056 | tf_op jit(solution)/shard_map/while/body/eval_jaxpr/sub | solution.py:31
  182.3 8.5 %fusion.54 = bf16[2,512,64]{1,2,0:T(8,128)(2,1)S(1)} fusion(bf16[4096,2,64]{0,2,1:T(8,128)(2,1)S(1)} %copy-done.2, f32[2,512,4096]{2,1,0:T(8,128)} %get-tuple-element.252, f32[2,512]{1,0:T(2,128)S(1)} %get-tuple-element.253), kind=kOutput, calls=%fused_computation.12.clone.1 | convolution fusion | flops 545325056 | bytes 17960960 | tf_op jit(solution)/shard_map/while/body/eval_jaxpr/hbk,khd->bhd/dot_general | solution.py:33
  191.8 0.7 iota_compare_fusion.4
  192.5 9.9 %fusion.53 = (f32[2,512]{1,0:T(2,128)S(1)}, f32[2,512,4096]{2,1,0:T(8,128)}) fusion(pred[4096]{0:T(1024)(128)(4,1)S(1)} %iota_compare_fusion.4, bf16[512,2,64]{0,2,1:T(8,128)(2,1)S(1)} %bitcast.77, bf16[4096,2,64]{0,2,1:T(8,128)(2,1)} %get-tuple-element.279), kind=kOutput, calls=%fused_computation.37.clone.1 | convolution fusion | flops 553652224 | bytes 17965056 | tf_op jit(solution)/shard_map/while/body/eval_jaxpr/sub | solution.py:31
  202.4 8.5 %fusion.54 = bf16[2,512,64]{1,2,0:T(8,128)(2,1)S(1)} fusion(bf16[4096,2,64]{0,2,1:T(8,128)(2,1)S(1)} %copy-done.2, f32[2,512,4096]{2,1,0:T(8,128)} %get-tuple-element.252, f32[2,512]{1,0:T(2,128)S(1)} %get-tuple-element.253), kind=kOutput, calls=%fused_computation.12.clone.1 | convolution fusion | flops 545325056 | bytes 17960960 | tf_op jit(solution)/shard_map/while/body/eval_jaxpr/hbk,khd->bhd/dot_general | solution.py:33
  211.8 0.7 iota_compare_fusion.4
  212.6 9.9 %fusion.53 = (f32[2,512]{1,0:T(2,128)S(1)}, f32[2,512,4096]{2,1,0:T(8,128)}) fusion(pred[4096]{0:T(1024)(128)(4,1)S(1)} %iota_compare_fusion.4, bf16[512,2,64]{0,2,1:T(8,128)(2,1)S(1)} %bitcast.77, bf16[4096,2,64]{0,2,1:T(8,128)(2,1)} %get-tuple-element.279), kind=kOutput, calls=%fused_computation.37.clone.1 | convolution fusion | flops 553652224 | bytes 17965056 | tf_op jit(solution)/shard_map/while/body/eval_jaxpr/sub | solution.py:31
  222.5 8.5 %fusion.54 = bf16[2,512,64]{1,2,0:T(8,128)(2,1)S(1)} fusion(bf16[4096,2,64]{0,2,1:T(8,128)(2,1)S(1)} %copy-done.2, f32[2,512,4096]{2,1,0:T(8,128)} %get-tuple-element.252, f32[2,512]{1,0:T(2,128)S(1)} %get-tuple-element.253), kind=kOutput, calls=%fused_computation.12.clone.1 | convolution fusion | flops 545325056 | bytes 17960960 | tf_op jit(solution)/shard_map/while/body/eval_jaxpr/hbk,khd->bhd/dot_general | solution.py:33
  231.9 0.7 iota_compare_fusion.4
  232.6 9.9 %fusion.53 = (f32[2,512]{1,0:T(2,128)S(1)}, f32[2,512,4096]{2,1,0:T(8,128)}) fusion(pred[4096]{0:T(1024)(128)(4,1)S(1)} %iota_compare_fusion.4, bf16[512,2,64]{0,2,1:T(8,128)(2,1)S(1)} %bitcast.77, bf16[4096,2,64]{0,2,1:T(8,128)(2,1)} %get-tuple-element.279), kind=kOutput, calls=%fused_computation.37.clone.1 | convolution fusion | flops 553652224 | bytes 17965056 | tf_op jit(solution)/shard_map/while/body/eval_jaxpr/sub | solution.py:31
  242.6 8.5 %fusion.54 = bf16[2,512,64]{1,2,0:T(8,128)(2,1)S(1)} fusion(bf16[4096,2,64]{0,2,1:T(8,128)(2,1)S(1)} %copy-done.2, f32[2,512,4096]{2,1,0:T(8,128)} %get-tuple-element.252, f32[2,512]{1,0:T(2,128)S(1)} %get-tuple-element.253), kind=kOutput, calls=%fused_computation.12.clone.1 | convolution fusion | flops 545325056 | bytes 17960960 | tf_op jit(solution)/shard_map/while/body/eval_jaxpr/hbk,khd->bhd/dot_general | solution.py:33
  252.7 9.9 %fusion.53 = (f32[2,512]{1,0:T(2,128)S(1)}, f32[2,512,4096]{2,1,0:T(8,128)}) fusion(pred[4096]{0:T(1024)(128)(4,1)S(1)} %iota_compare_fusion.4, bf16[512,2,64]{0,2,1:T(8,128)(2,1)S(1)} %bitcast.77, bf16[4096,2,64]{0,2,1:T(8,128)(2,1)} %get-tuple-element.279), kind=kOutput, calls=%fused_computation.37.clone.1 | convolution fusion | flops 553652224 | bytes 17965056 | tf_op jit(solution)/shard_map/while/body/eval_jaxpr/sub | solution.py:31
  262.6 8.5 %fusion.54 = bf16[2,512,64]{1,2,0:T(8,128)(2,1)S(1)} fusion(bf16[4096,2,64]{0,2,1:T(8,128)(2,1)S(1)} %copy-done.2, f32[2,512,4096]{2,1,0:T(8,128)} %get-tuple-element.252, f32[2,512]{1,0:T(2,128)S(1)} %get-tuple-element.253), kind=kOutput, calls=%fused_computation.12.clone.1 | convolution fusion | flops 545325056 | bytes 17960960 | tf_op jit(solution)/shard_map/while/body/eval_jaxpr/hbk,khd->bhd/dot_general | solution.py:33
  272.8 9.9 %fusion.53 = (f32[2,512]{1,0:T(2,128)S(1)}, f32[2,512,4096]{2,1,0:T(8,128)}) fusion(pred[4096]{0:T(1024)(128)(4,1)S(1)} %iota_compare_fusion.4, bf16[512,2,64]{0,2,1:T(8,128)(2,1)S(1)} %bitcast.77, bf16[4096,2,64]{0,2,1:T(8,128)(2,1)} %get-tuple-element.279), kind=kOutput, calls=%fused_computation.37.clone.1 | convolution fusion | flops 553652224 | bytes 17965056 | tf_op jit(solution)/shard_map/while/body/eval_jaxpr/sub | solution.py:31
  282.7 8.5 %fusion.54 = bf16[2,512,64]{1,2,0:T(8,128)(2,1)S(1)} fusion(bf16[4096,2,64]{0,2,1:T(8,128)(2,1)S(1)} %copy-done.2, f32[2,512,4096]{2,1,0:T(8,128)} %get-tuple-element.252, f32[2,512]{1,0:T(2,128)S(1)} %get-tuple-element.253), kind=kOutput, calls=%fused_computation.12.clone.1 | convolution fusion | flops 545325056 | bytes 17960960 | tf_op jit(solution)/shard_map/while/body/eval_jaxpr/hbk,khd->bhd/dot_general | solution.py:33
  292.9 9.9 %fusion.53 = (f32[2,512]{1,0:T(2,128)S(1)}, f32[2,512,4096]{2,1,0:T(8,128)}) fusion(pred[4096]{0:T(1024)(128)(4,1)S(1)} %iota_compare_fusion.4, bf16[512,2,64]{0,2,1:T(8,128)(2,1)S(1)} %bitcast.77, bf16[4096,2,64]{0,2,1:T(8,128)(2,1)} %get-tuple-element.279), kind=kOutput, calls=%fused_computation.37.clone.1 | convolution fusion | flops 553652224 | bytes 17965056 | tf_op jit(solution)/shard_map/while/body/eval_jaxpr/sub | solution.py:31
  302.8 8.5 %fusion.54 = bf16[2,512,64]{1,2,0:T(8,128)(2,1)S(1)} fusion(bf16[4096,2,64]{0,2,1:T(8,128)(2,1)S(1)} %copy-done.2, f32[2,512,4096]{2,1,0:T(8,128)} %get-tuple-element.252, f32[2,512]{1,0:T(2,128)S(1)} %get-tuple-element.253), kind=kOutput, calls=%fused_computation.12.clone.1 | convolution fusion | flops 545325056 | bytes 17960960 | tf_op jit(solution)/shard_map/while/body/eval_jaxpr/hbk,khd->bhd/dot_general | solution.py:33
  312.9 9.9 %fusion.53 = (f32[2,512]{1,0:T(2,128)S(1)}, f32[2,512,4096]{2,1,0:T(8,128)}) fusion(pred[4096]{0:T(1024)(128)(4,1)S(1)} %iota_compare_fusion.4, bf16[512,2,64]{0,2,1:T(8,128)(2,1)S(1)} %bitcast.77, bf16[4096,2,64]{0,2,1:T(8,128)(2,1)} %get-tuple-element.279), kind=kOutput, calls=%fused_computation.37.clone.1 | convolution fusion | flops 553652224 | bytes 17965056 | tf_op jit(solution)/shard_map/while/body/eval_jaxpr/sub | solution.py:31
  322.9 8.5 %fusion.54 = bf16[2,512,64]{1,2,0:T(8,128)(2,1)S(1)} fusion(bf16[4096,2,64]{0,2,1:T(8,128)(2,1)S(1)} %copy-done.2, f32[2,512,4096]{2,1,0:T(8,128)} %get-tuple-element.252, f32[2,512]{1,0:T(2,128)S(1)} %get-tuple-element.253), kind=kOutput, calls=%fused_computation.12.clone.1 | convolution fusion | flops 545325056 | bytes 17960960 | tf_op jit(solution)/shard_map/while/body/eval_jaxpr/hbk,khd->bhd/dot_general | solution.py:33
  332.2 8.1 %all-to-all-start.3 = ((bf16[32,128,128]{2,1,0:T(8,128)(2,1)}), bf16[32,128,128]{2,1,0:T(8,128)(2,1)S(1)}, u32[]{:S(2)}, u32[]{:S(2)}) async-start(bf16[32,128,128]{2,1,0:T(8,128)(2,1)} %bitcast.81), calls=%async_computation.3 | async-start | bytes 2097152 | tf_op jit(solution)/shard_map/all_to_all | solution.py:51
  340.9 0.8 bitcast_select_fusion
  341.7 27.6 %all-to-all-done.3 = bf16[32,128,128]{2,1,0:T(8,128)(2,1)S(1)} async-done(((bf16[32,128,128]{2,1,0:T(8,128)(2,1)}), bf16[32,128,128]{2,1,0:T(8,128)(2,1)S(1)}, u32[]{:S(2)}, u32[]{:S(2)}) %all-to-all-start.3) | async-done | bytes 1048608 | tf_op jit(solution)/shard_map/all_to_all | solution.py:51
  370.0 1.3 copy.53
  (81 shorter events, 15.5 us)
Async XLA Ops:
  0.6 78.4 %copy-start = (bf16[32,4096]{1,0:T(8,128)(2,1)S(1)}, bf16[32,4096]{1,0:T(8,128)(2,1)}, u32[]{:S(2)}) copy-start(bf16[32,4096]{1,0:T(8,128)(2,1)} %param.13) | copy-start | bytes 786436
  3.0 39.0 %all-to-all-start.1 = ((bf16[128,32,128]{0,2,1:T(8,128)(2,1)}), bf16[128,32,128]{0,2,1:T(8,128)(2,1)S(1)}, u32[]{:S(2)}, u32[]{:S(2)}) async-start(bf16[128,32,128]{0,2,1:T(8,128)(2,1)} %bitcast.3), calls=%async_computation.1 | async-start | bytes 2097152 | tf_op jit(solution)/shard_map/all_to_all | solution.py:47
  41.9 33.2 %all-to-all-start.2 = ((bf16[128,32,128]{0,2,1:T(8,128)(2,1)}), bf16[128,32,128]{0,2,1:T(8,128)(2,1)S(1)}, u32[]{:S(2)}, u32[]{:S(2)}) async-start(bf16[128,32,128]{0,2,1:T(8,128)(2,1)} %bitcast.5), calls=%async_computation.2 | async-start | bytes 2097152 | tf_op jit(solution)/shard_map/all_to_all | solution.py:48
  75.1 33.2 %all-to-all-start = ((bf16[128,32,128]{0,2,1:T(8,128)(2,1)}), bf16[128,32,128]{0,2,1:T(8,128)(2,1)S(1)}, u32[]{:S(2)}, u32[]{:S(2)}) async-start(bf16[128,32,128]{0,2,1:T(8,128)(2,1)} %bitcast.74), calls=%async_computation | async-start | bytes 2097152 | tf_op jit(solution)/shard_map/all_to_all | solution.py:46
  108.3 16.9 %all-to-all-start.4 = ((bf16[32,32,128]{2,0,1:T(8,128)(2,1)}), bf16[32,32,128]{2,0,1:T(8,128)(2,1)}, u32[]{:S(2)}, u32[]{:S(2)}) async-start(bf16[32,32,128]{2,0,1:T(8,128)(2,1)} %copy_bitcast_fusion), calls=%async_computation.4 | async-start | bytes 524288 | tf_op jit(solution)/shard_map/all_to_all | solution.py:52
  125.2 11.7 %copy-start.1 = (bf16[4096,2,64]{0,2,1:T(8,128)(2,1)S(1)}, bf16[4096,2,64]{0,2,1:T(8,128)(2,1)}, u32[]{:S(2)}) copy-start(bf16[4096,2,64]{0,2,1:T(8,128)(2,1)} %get-tuple-element.301) | copy-start | bytes 3145732 | tf_op jit(solution)/shard_map/while
  136.9 8.7 %copy-start.3 = (bf16[2,512,128]{2,1,0:T(8,128)(2,1)S(1)}, bf16[2,512,128]{2,1,0:T(8,128)(2,1)}, u32[]{:S(2)}) copy-start(bf16[2,512,128]{2,1,0:T(8,128)(2,1)} %get-tuple-element.291) | copy-start | bytes 786436 | tf_op jit(solution)/shard_map/while
  145.6 0.7 copy-start.4
  146.3 11.7 %copy-start.1 = (bf16[4096,2,64]{0,2,1:T(8,128)(2,1)S(1)}, bf16[4096,2,64]{0,2,1:T(8,128)(2,1)}, u32[]{:S(2)}) copy-start(bf16[4096,2,64]{0,2,1:T(8,128)(2,1)} %get-tuple-element.301) | copy-start | bytes 3145732 | tf_op jit(solution)/shard_map/while
  158.0 8.7 %copy-start.3 = (bf16[2,512,128]{2,1,0:T(8,128)(2,1)S(1)}, bf16[2,512,128]{2,1,0:T(8,128)(2,1)}, u32[]{:S(2)}) copy-start(bf16[2,512,128]{2,1,0:T(8,128)(2,1)} %get-tuple-element.291) | copy-start | bytes 786436 | tf_op jit(solution)/shard_map/while
  166.7 0.7 copy-start.4
  167.4 164.7 %all-to-all-start.5 = ((bf16[32,32,128]{2,1,0:T(8,128)(2,1)}), bf16[32,32,128]{2,1,0:T(8,128)(2,1)S(1)}, u32[]{:S(2)}, u32[]{:S(2)}) async-start(bf16[32,32,128]{2,1,0:T(8,128)(2,1)} %bitcast.82), calls=%async_computation.5 | async-start | bytes 524288 | tf_op jit(solution)/shard_map/all_to_all | solution.py:54
  171.5 10.8 %copy-start.2 = (bf16[4096,2,64]{0,2,1:T(8,128)(2,1)S(1)}, bf16[4096,2,64]{0,2,1:T(8,128)(2,1)}, u32[]{:S(2)}) copy-start(bf16[4096,2,64]{0,2,1:T(8,128)(2,1)} %get-tuple-element.280) | copy-start | bytes 3145732 | tf_op jit(solution)/shard_map/while
  191.6 10.8 %copy-start.2 = (bf16[4096,2,64]{0,2,1:T(8,128)(2,1)S(1)}, bf16[4096,2,64]{0,2,1:T(8,128)(2,1)}, u32[]{:S(2)}) copy-start(bf16[4096,2,64]{0,2,1:T(8,128)(2,1)} %get-tuple-element.280) | copy-start | bytes 3145732 | tf_op jit(solution)/shard_map/while
  211.7 10.8 %copy-start.2 = (bf16[4096,2,64]{0,2,1:T(8,128)(2,1)S(1)}, bf16[4096,2,64]{0,2,1:T(8,128)(2,1)}, u32[]{:S(2)}) copy-start(bf16[4096,2,64]{0,2,1:T(8,128)(2,1)} %get-tuple-element.280) | copy-start | bytes 3145732 | tf_op jit(solution)/shard_map/while
  231.8 10.8 %copy-start.2 = (bf16[4096,2,64]{0,2,1:T(8,128)(2,1)S(1)}, bf16[4096,2,64]{0,2,1:T(8,128)(2,1)}, u32[]{:S(2)}) copy-start(bf16[4096,2,64]{0,2,1:T(8,128)(2,1)} %get-tuple-element.280) | copy-start | bytes 3145732 | tf_op jit(solution)/shard_map/while
  251.8 10.8 %copy-start.2 = (bf16[4096,2,64]{0,2,1:T(8,128)(2,1)S(1)}, bf16[4096,2,64]{0,2,1:T(8,128)(2,1)}, u32[]{:S(2)}) copy-start(bf16[4096,2,64]{0,2,1:T(8,128)(2,1)} %get-tuple-element.280) | copy-start | bytes 3145732 | tf_op jit(solution)/shard_map/while
  271.9 10.8 %copy-start.2 = (bf16[4096,2,64]{0,2,1:T(8,128)(2,1)S(1)}, bf16[4096,2,64]{0,2,1:T(8,128)(2,1)}, u32[]{:S(2)}) copy-start(bf16[4096,2,64]{0,2,1:T(8,128)(2,1)} %get-tuple-element.280) | copy-start | bytes 3145732 | tf_op jit(solution)/shard_map/while
  292.0 10.8 %copy-start.2 = (bf16[4096,2,64]{0,2,1:T(8,128)(2,1)S(1)}, bf16[4096,2,64]{0,2,1:T(8,128)(2,1)}, u32[]{:S(2)}) copy-start(bf16[4096,2,64]{0,2,1:T(8,128)(2,1)} %get-tuple-element.280) | copy-start | bytes 3145732 | tf_op jit(solution)/shard_map/while
  312.1 10.8 %copy-start.2 = (bf16[4096,2,64]{0,2,1:T(8,128)(2,1)S(1)}, bf16[4096,2,64]{0,2,1:T(8,128)(2,1)}, u32[]{:S(2)}) copy-start(bf16[4096,2,64]{0,2,1:T(8,128)(2,1)} %get-tuple-element.280) | copy-start | bytes 3145732 | tf_op jit(solution)/shard_map/while
  332.2 37.2 %all-to-all-start.3 = ((bf16[32,128,128]{2,1,0:T(8,128)(2,1)}), bf16[32,128,128]{2,1,0:T(8,128)(2,1)S(1)}, u32[]{:S(2)}, u32[]{:S(2)}) async-start(bf16[32,128,128]{2,1,0:T(8,128)(2,1)} %bitcast.81), calls=%async_computation.3 | async-start | bytes 2097152 | tf_op jit(solution)/shard_map/all_to_all | solution.py:51
where the time goes:
time: 373 us; the launch traced here: 371 us
  matrix products  184 us (49%)
  waiting for transfers between devices  116 us (31%)
  starting transfers between devices  34.5 us (9%)
  local copies, waits for them, and re-layouts  27.4 us (7%)
  other arithmetic  7.93 us (2%)
    sub x10, matrix products, one_block(): weights = jnp.exp(scores - row_max)  99.2 us
    dot_general x10, matrix products, one_block(): jnp.einsum('hbk,khd->bhd', weights, value_heads, preferred_element_type=j...  84.9 us
    all_to_all x1, waiting for transfers between devices, on_device(): lax.all_to_all(enc_query, 'seq', split_axis=1, concat_axis=0, tiled=True)  28.5 us
    all_to_all x1, waiting for transfers between devices, on_device(): lax.all_to_all(heads_mixed, 'seq', split_axis=0, concat_axis=1, tiled=True)  27.6 us
    all_to_all x1, waiting for transfers between devices, on_device(): lax.all_to_all(enc_value, 'seq', split_axis=1, concat_axis=0, tiled=True)  27 us
    all_to_all x1, waiting for transfers between devices, on_device(): lax.all_to_all(enc_key, 'seq', split_axis=1, concat_axis=0, tiled=True)  26.9 us
    all_to_all x1, starting transfers between devices, on_device(): lax.all_to_all(enc_key, 'seq', split_axis=1, concat_axis=0, tiled=True)  9.87 us
    unnamed x6, local copies, waits for them, and re-layouts  8.14 us
  transfers between devices with their start and end apart: 6, of which 5 were waited for; matrix products, arithmetic and copies ran while one was open for 47% of the time, Pallas kernels for 0%

commit v1 on v0

v1 whole, which is shorter than its diff:
```python
import math

import jax
import jax.numpy as jnp
from jax import lax
from jax.experimental import pallas as pl
from jax.experimental.pallas import tpu as pltpu
from jax.sharding import PartitionSpec as P

DH = 64
LANES = 128
SCALE = 0.125
EXP2_SCALE = SCALE * math.log2(math.e)
SUM_LOW, SUM_HIGH = 2.0**-60, 2.0**100
QUERY_BLOCK = 512
KEY_BLOCK = 4096
SLOW_KEYS = 512
VMEM_BYTES = 56 << 20
CONTRACT_LAST = (((1,), (1,)), ((), ()))


def prepare_kernel(length_ref, kv_ref, key_ref, value_ref):
    length = length_ref[0]
    sources = kv_ref.shape[0]
    rows = kv_ref.shape[1] // 2
    group = max(1, 512 // rows)

    def step(g, carry):
        keys = kv_ref[pl.ds(g * group, group), :rows, :].reshape(group * rows, LANES)
        values = kv_ref[pl.ds(g * group, group), rows:, :].reshape(group * rows, LANES)
        start = pl.multiple_of(g * group * rows, group * rows)
        position = start + lax.broadcasted_iota(jnp.int32, (group * rows, LANES), 0)
        live = position < length
        first_key = kv_ref[0, 0:1, :]
        key_ref[pl.ds(start, group * rows), :] = jnp.where(live, keys, first_key)
        flipped = jnp.where(live, values, jnp.zeros_like(values)).astype(jnp.float32).T
        flipped = flipped.astype(jnp.bfloat16)
        along = start + lax.broadcasted_iota(jnp.int32, (16, group * rows), 1)
        ones = jnp.where(along < length, 1.0, 0.0).astype(jnp.bfloat16)
        for head in range(2):
            value_ref[head, :DH, pl.ds(start, group * rows)] = flipped[head * DH : (head + 1) * DH]
            value_ref[head, DH:, pl.ds(start, group * rows)] = ones
        return carry

    lax.fori_loop(0, sources // group, step, 0)


def prepare(valid_len, kv):
    keys = kv.shape[0] * kv.shape[1] // 2
    vmem = pl.BlockSpec(memory_space=pltpu.VMEM)
    return pl.pallas_call(
        prepare_kernel,
        in_specs=[pl.BlockSpec(memory_space=pltpu.SMEM), vmem],
        out_specs=[vmem, vmem],
        out_shape=[
            jax.ShapeDtypeStruct((keys, LANES), jnp.bfloat16),
            jax.ShapeDtypeStruct((2, DH + 16, keys), jnp.bfloat16),
        ],
        compiler_params=pltpu.CompilerParams(vmem_limit_bytes=VMEM_BYTES),
        cost_estimate=pl.CostEstimate(flops=0, bytes_accessed=6 << 20, transcendentals=0),
    )(valid_len, kv)


def attend_kernel(query_ref, key_ref, value_ref, out_ref, score_ref):
    keys = key_ref.shape[0]
    lane = lax.broadcasted_iota(jnp.int32, (QUERY_BLOCK, LANES), 1)

    def head_queries(queries):
        zeros = jnp.zeros_like(queries)
        return [jnp.where(lane < DH, queries, zeros), jnp.where(lane < DH, zeros, queries)]

    def scores(queries, start, count):
        return lax.dot_general(
            key_ref[pl.ds(start, count), :], queries, CONTRACT_LAST, preferred_element_type=jnp.float32
        )

    def weigh(head, weights, start, count):
        return jnp.dot(
            value_ref[head, :, pl.ds(start, count)],
            weights.astype(jnp.bfloat16),
            preferred_element_type=jnp.float32,
        )

    def store(rows, totals):
        mixed = jnp.concatenate([t[:DH] / t[DH : DH + 1] for t in totals], axis=0)
        out_ref[rows, :] = mixed.T.astype(jnp.bfloat16)

    def block(index, carry):
        rows = pl.ds(pl.multiple_of(index * QUERY_BLOCK, QUERY_BLOCK), QUERY_BLOCK)
        queries = head_queries(query_ref[rows, :])
        totals = []
        for head in range(2):
            total = None
            for start in range(0, keys, KEY_BLOCK):
                weights = jnp.exp2(scores(queries[head], start, KEY_BLOCK) * EXP2_SCALE)
                part = weigh(head, weights, start, KEY_BLOCK)
                total = part if total is None else total + part
            totals.append(total)
        store(rows, totals)
        sums = jnp.concatenate([t[DH : DH + 8] for t in totals], axis=0)
        safe = jnp.logical_and(sums >= SUM_LOW, sums <= SUM_HIGH)
        unsafe = jnp.max(jnp.where(safe, 0.0, 1.0)) > 0.0

        @pl.when(unsafe)
        def _():
            totals = []
            for head in range(2):

                def first(i, top):
                    start = pl.multiple_of(i * SLOW_KEYS, SLOW_KEYS)
                    found = scores(queries[head], start, SLOW_KEYS)
                    score_ref[pl.ds(start, SLOW_KEYS), :] = found
                    return jnp.maximum(top, jnp.max(found, axis=0, keepdims=True))

                top = lax.fori_loop(
                    0, keys // SLOW_KEYS, first, jnp.full((1, QUERY_BLOCK), -jnp.inf, jnp.float32)
                )

                def second(i, total):
                    start = pl.multiple_of(i * SLOW_KEYS, SLOW_KEYS)
                    found = score_ref[pl.ds(start, SLOW_KEYS), :]
                    return total + weigh(head, jnp.exp2((found - top) * EXP2_SCALE), start, SLOW_KEYS)

                totals.append(
                    lax.fori_loop(
                        0, keys // SLOW_KEYS, second, jnp.zeros((DH + 16, QUERY_BLOCK), jnp.float32)
                    )
                )
            store(rows, totals)

        return carry

    lax.fori_loop(0, query_ref.shape[0] // QUERY_BLOCK, block, 0)


def attend(queries, keys, values):
    sources, rows, _ = queries.shape
    total, count = sources * rows, keys.shape[0]
    vmem = pl.BlockSpec(memory_space=pltpu.VMEM)
    result = pl.pallas_call(
        attend_kernel,
        in_specs=[vmem, vmem, vmem],
        out_specs=vmem,
        out_shape=jax.ShapeDtypeStruct((total, LANES), jnp.bfloat16),
        scratch_shapes=[pltpu.VMEM((count, QUERY_BLOCK), jnp.float32)],
        compiler_params=pltpu.CompilerParams(vmem_limit_bytes=VMEM_BYTES),
        cost_estimate=pl.CostEstimate(
            flops=total * count * 2 * 512 * 2, bytes_accessed=4 << 20, transcendentals=total * count * 2
        ),
    )(queries.reshape(total, LANES), keys, values)
    return result.reshape(sources, rows, LANES)


def by_owner(rows):
    return rows.reshape(rows.shape[0], -1, LANES).transpose(1, 0, 2)


def by_row(blocks):
    return blocks.transpose(1, 0, 2).reshape(blocks.shape[1], -1)


def exchange(blocks):
    return lax.all_to_all(blocks, "seq", split_axis=0, concat_axis=0, tiled=True)


def on_device(enc_query, enc_key, enc_value, dec_query, enc_length, tgt_length):
    rows_local = dec_query.shape[0]
    kv = exchange(by_owner(jnp.concatenate([enc_key, enc_value], axis=0)))
    cuts = (0, 32, 96, 128)
    sent = [by_owner(enc_query[a:b]) for a, b in zip(cuts, cuts[1:])]
    sent[0] = jnp.concatenate([by_owner(dec_query), sent[0]], axis=1)
    arrived = [exchange(s) for s in sent]
    keys, values = prepare(enc_length, kv)
    returned = [exchange(attend(q, keys, values)) for q in arrived]
    returned_cross, returned[0] = returned[0][:, :rows_local], returned[0][:, rows_local:]
    enc_mixed = jnp.concatenate([by_row(r) for r in returned], axis=0)
    first_row = lax.axis_index("seq") * rows_local
    keep_rows = first_row + jnp.arange(rows_local, dtype=jnp.int32) < tgt_length[0]
    crossed = by_row(returned_cross)
    cross_mixed = jnp.where(keep_rows[:, None], crossed, jnp.zeros_like(crossed))
    return (enc_mixed, cross_mixed)


def solution(mesh):
    return jax.shard_map(
        on_device,
        mesh=mesh,
        in_specs=(
            P(("dp", "seq"), None),
            P(("dp", "seq"), None),
            P(("dp", "seq"), None),
            P(("dp", "seq"), None),
            P("dp"),
            P("dp"),
        ),
        out_specs=(P(("dp", "seq"), None), P(("dp", "seq"), None)),
        check_vma=False,
    )
```

time: 373 us -> 234 us (0.63)
  matrix products: 184 us -> 0 us
  Pallas kernels: 0 us -> 80.4 us
  waiting for transfers between devices: 116 us -> 90.8 us
  local copies, waits for them, and re-layouts: 27.4 us -> 8.65 us
  starting transfers between devices: 34.5 us -> 47.4 us
  other arithmetic: 7.93 us -> 4.15 us
    sub x10 -> x0, matrix products: 99.2 us -> none  [one_block(): weights = jnp.exp(scores - row_max)]
    dot_general x10 -> x0, matrix products: 84.9 us -> none  [one_block(): jnp.einsum('hbk,khd->bhd', weights, value_heads, preferred_element_type=j...]
    pallas_call x0 -> x4, Pallas kernels: none -> 80.4 us  [the longest x3 76.4 us: attend(): pl.pallas_call(attend_kernel, in_specs=[vmem, vmem, vmem], out_specs=vmem...]
    all_to_all x6 -> x7, waiting for transfers between devices: 116 us -> 90.8 us  [exchange(): lax.all_to_all(blocks, 'seq', split_axis=0, concat_axis=0, tiled=True)]
    all_to_all x6 -> x7, starting transfers between devices: 34.5 us -> 47.4 us  [exchange(): lax.all_to_all(blocks, 'seq', split_axis=0, concat_axis=0, tiled=True)]
    lt x10 -> x0, other arithmetic: 7.1 us -> none  [attend_block(): live_keys = jnp.arange(key_rows, dtype=jnp.int32) < valid_len]
    dynamic_update_slice x20 -> x0, local copies, waits for them, and re-layouts: 6.65 us -> none  [attend_block(): lax.map(one_block, queries.reshape(blocks_num, row_block, col_width))]
    all_to_all x5 -> x0, local copies, waits for them, and re-layouts: 4.39 us -> none  [the longest x1 1.64 us: on_device(): lax.all_to_all(enc_key, 'seq', split_axis=1, concat_axis=0, tiled=True)]
  transfers between devices with their start and end apart: 6 -> 7, of which waited for: 5 -> 4; matrix products, arithmetic and copies ran while one was open for 47% -> 4% of each run, Pallas kernels for 0% -> 34%
where the time goes in v1:
time: 234 us; the launch traced here: 233 us
  waiting for transfers between devices  90.8 us (39%)
  Pallas kernels  80.4 us (34%)
  starting transfers between devices  47.4 us (20%)
  local copies, waits for them, and re-layouts  8.65 us (4%)
  other arithmetic  4.15 us (2%)
    all_to_all x7, waiting for transfers between devices, exchange(): lax.all_to_all(blocks, 'seq', split_axis=0, concat_axis=0, tiled=True)  90.8 us
    pallas_call x3, Pallas kernels, attend(): pl.pallas_call(attend_kernel, in_specs=[vmem, vmem, vmem], out_specs=vmem...  76.4 us
    all_to_all x7, starting transfers between devices, exchange(): lax.all_to_all(blocks, 'seq', split_axis=0, concat_axis=0, tiled=True)  47.4 us
  transfers between devices with their start and end apart: 7, of which 4 were waited for; matrix products, arithmetic and copies ran while one was open for 4% of the time, Pallas kernels for 34%

profile of v1, /device:TPU:2, one launch (start us, length us, event | category | flops | bytes accessed | tf_op | source)
XLA Modules:
  0.0 233.5 jit_solution(13581479010358589162)
XLA Ops:
  0.6 0.0 copy-start
  0.6 1.1 slice_bitcast_fusion.4
  1.8 0.0 copy-start.2
  1.8 0.7 copy.44
  2.5 9.9 %all-to-all-start.5 = ((bf16[32,32,128]{2,1,0:T(8,128)(2,1)}), bf16[32,32,128]{2,1,0:T(8,128)(2,1)S(1)}, u32[]{:S(2)}, u32[]{:S(2)}) async-start(bf16[32,32,128]{2,1,0:T(8,128)(2,1)} %bitcast.59), calls=%async_computation.5 | async-start | bytes 524288 | tf_op jit(solution)/shard_map/all_to_all | solution.py:163
  12.5 0.0 copy-done
  12.5 0.0 copy-start.3
  12.5 0.9 pad_maximum_fusion.2
  13.4 11.2 %all-to-all-done.5 = bf16[32,32,128]{2,1,0:T(8,128)(2,1)S(1)} async-done(((bf16[32,32,128]{2,1,0:T(8,128)(2,1)}), bf16[32,32,128]{2,1,0:T(8,128)(2,1)S(1)}, u32[]{:S(2)}, u32[]{:S(2)}) %all-to-all-start.5) | async-done | bytes 262176 | tf_op jit(solution)/shard_map/all_to_all | solution.py:163
  24.6 0.0 copy-start.6
  24.6 0.7 copy-done.6
  25.3 4.6 %all-to-all-start = ((bf16[32,64,128]{2,1,0:T(8,128)(2,1)}), bf16[32,64,128]{2,1,0:T(8,128)(2,1)}, u32[]{:S(2)}, u32[]{:S(2)}) async-start(bf16[32,64,128]{2,1,0:T(8,128)(2,1)} %pad_maximum_fusion.2), calls=%async_computation | async-start | bytes 1048576 | tf_op jit(solution)/shard_map/all_to_all | solution.py:163
  29.9 0.0 copy-done.2
  29.9 0.7 copy.18
  30.6 0.0 copy-done.3
  30.6 1.3 copy.19
  31.9 1.5 pad_maximum_fusion
  33.4 2.9 %copy.20 = bf16[256,32,128]{2,0,1:T(8,128)(2,1)} copy(bf16[256,32,128]{0,2,1:T(8,128)(2,1)S(1)} %bitcast.64) | data formatting | bytes 4194304 | tf_op jit(solution)/shard_map/reshape | solution.py:155
  36.3 11.7 %all-to-all-done = bf16[32,64,128]{2,1,0:T(8,128)(2,1)} async-done(((bf16[32,64,128]{2,1,0:T(8,128)(2,1)}), bf16[32,64,128]{2,1,0:T(8,128)(2,1)}, u32[]{:S(2)}, u32[]{:S(2)}) %all-to-all-start) | async-done | bytes 524320 | tf_op jit(solution)/shard_map/all_to_all | solution.py:163
  47.9 0.0 copy-start.4
  47.9 4.1 %all-to-all-start.1 = ((bf16[32,256,128]{2,1,0:T(8,128)(2,1)}), bf16[32,256,128]{2,1,0:T(8,128)(2,1)S(1)}, u32[]{:S(2)}, u32[]{:S(2)}) async-start(bf16[32,256,128]{2,1,0:T(8,128)(2,1)} %bitcast.63), calls=%async_computation.1 | async-start | bytes 4194304 | tf_op jit(solution)/shard_map/all_to_all | solution.py:163
  52.1 0.0 copy-done.4
  52.1 0.9 bitcast_bitcast_fusion
  53.0 50.7 %all-to-all-done.1.kv_ref = bf16[32,256,128]{2,1,0:T(8,128)(2,1)S(1)} async-done(((bf16[32,256,128]{2,1,0:T(8,128)(2,1)}), bf16[32,256,128]{2,1,0:T(8,128)(2,1)S(1)}, u32[]{:S(2)}, u32[]{:S(2)}) %all-to-all-start.1) | async-done | bytes 2097184 | tf_op jit(solution)/shard_map/all_to_all | solution.py:163
  103.8 0.0 copy-start.1
  103.8 3.9 %all-to-all-start.3 = ((bf16[32,64,128]{2,1,0:T(8,128)(2,1)}), bf16[32,64,128]{2,1,0:T(8,128)(2,1)S(1)}, u32[]{:S(2)}, u32[]{:S(2)}) async-start(bf16[32,64,128]{2,1,0:T(8,128)(2,1)} %bitcast_bitcast_fusion), calls=%async_computation.3 | async-start | bytes 1048576 | tf_op jit(solution)/shard_map/all_to_all | solution.py:163
  109.0 0.0 copy-done.1
  109.0 4.0 %shard_map.77 = (bf16[4096,128]{1,0:T(8,128)(2,1)}, bf16[2,80,4096]{2,1,0:T(8,128)(2,1)}) custom-call(s32[1]{0:T(128)S(6)} %copy.46.length_ref, bf16[32,256,128]{2,1,0:T(8,128)(2,1)} %copy-done.1), custom_call_target="tpu_custom_call" | custom-call | bytes 6291456 | tf_op jit(solution)/shard_map/pallas_call | solution.py:51
  113.0 20.2 %shard_map.80 = bf16[1024,128]{1,0:T(8,128)(2,1)} custom-call(bf16[1024,128]{1,0:T(8,128)(2,1)} %bitcast.70, bf16[4096,128]{1,0:T(8,128)(2,1)} %get-tuple-element.4.key_ref, bf16[2,80,4096]{2,1,0:T(8,128)(2,1)} %get-tuple-element.5.value_ref), custom_call_target="tpu_custom_call" | custom-call | flops 8589934592 | bytes 4194304 | tf_op jit(solution)/shard_map/pallas_call | solution.py:140
  133.2 0.0 all-to-all-done.3
  133.2 0.0 copy-start.5
  133.2 8.4 %all-to-all-start.6 = ((bf16[32,32,128]{2,1,0:T(8,128)(2,1)}), bf16[32,32,128]{2,1,0:T(8,128)(2,1)S(1)}, u32[]{:S(2)}, u32[]{:S(2)}) async-start(bf16[32,32,128]{2,1,0:T(8,128)(2,1)} %bitcast.71), calls=%async_computation.6 | async-start | bytes 524288 | tf_op jit(solution)/shard_map/all_to_all | solution.py:163
  141.6 28.1 %shard_map.78 = bf16[2048,128]{1,0:T(8,128)(2,1)} custom-call(bf16[2048,128]{1,0:T(8,128)(2,1)} %bitcast.2.query_ref, bf16[4096,128]{1,0:T(8,128)(2,1)} %get-tuple-element.4.key_ref, bf16[2,80,4096]{2,1,0:T(8,128)(2,1)} %get-tuple-element.5.value_ref), custom_call_target="tpu_custom_call" | custom-call | flops 17179869184 | bytes 4194304 | tf_op jit(solution)/shard_map/pallas_call | solution.py:140
  169.7 0.0 copy-done.5
  169.7 0.0 all-to-all-done.6
  169.7 8.1 %all-to-all-start.2 = ((bf16[32,64,128]{2,1,0:T(8,128)(2,1)}), bf16[32,64,128]{2,1,0:T(8,128)(2,1)S(1)}, u32[]{:S(2)}, u32[]{:S(2)}) async-start(bf16[32,64,128]{2,1,0:T(8,128)(2,1)} %bitcast.69), calls=%async_computation.2 | async-start | bytes 1048576 | tf_op jit(solution)/shard_map/all_to_all | solution.py:163
  177.9 28.1 %shard_map.79 = bf16[2048,128]{1,0:T(8,128)(2,1)} custom-call(bf16[2048,128]{1,0:T(8,128)(2,1)} %bitcast.67, bf16[4096,128]{1,0:T(8,128)(2,1)} %get-tuple-element.4.key_ref, bf16[2,80,4096]{2,1,0:T(8,128)(2,1)} %get-tuple-element.5.value_ref), custom_call_target="tpu_custom_call" | custom-call | flops 17179869184 | bytes 4194304 | tf_op jit(solution)/shard_map/pallas_call | solution.py:140
  206.0 0.0 all-to-all-done.2
  206.0 8.3 %all-to-all-start.4 = ((bf16[32,64,128]{2,1,0:T(8,128)(2,1)}), bf16[32,64,128]{2,1,0:T(8,128)(2,1)S(1)}, u32[]{:S(2)}, u32[]{:S(2)}) async-start(bf16[32,64,128]{2,1,0:T(8,128)(2,1)} %bitcast.68), calls=%async_computation.4 | async-start | bytes 1048576 | tf_op jit(solution)/shard_map/all_to_all | solution.py:163
  214.4 0.8 bitcast_select_fusion
  215.2 17.1 %all-to-all-done.4 = bf16[32,64,128]{2,1,0:T(8,128)(2,1)S(1)} async-done(((bf16[32,64,128]{2,1,0:T(8,128)(2,1)}), bf16[32,64,128]{2,1,0:T(8,128)(2,1)S(1)}, u32[]{:S(2)}, u32[]{:S(2)}) %all-to-all-start.4) | async-done | bytes 524320 | tf_op jit(solution)/shard_map/all_to_all | solution.py:163
  232.3 0.1 copy_bitcast_fusion
  232.4 1.0 pad_maximum_fusion.1
  (6 shorter events, 0.2 us)
Async XLA Ops:
  0.6 11.8 %copy-start = (bf16[32,4096]{1,0:T(8,128)(2,1)S(1)}, bf16[32,4096]{1,0:T(8,128)(2,1)}, u32[]{:S(2)}) copy-start(bf16[32,4096]{1,0:T(8,128)(2,1)} %param.9) | copy-start | bytes 786436
  1.8 28.2 %copy-start.2 = (bf16[128,4096]{1,0:T(8,128)(2,1)S(1)}, bf16[128,4096]{1,0:T(8,128)(2,1)}, u32[]{:S(2)}) copy-start(bf16[128,4096]{1,0:T(8,128)(2,1)} %param.7) | copy-start | bytes 3145732
  2.5 22.1 %all-to-all-start.5 = ((bf16[32,32,128]{2,1,0:T(8,128)(2,1)}), bf16[32,32,128]{2,1,0:T(8,128)(2,1)S(1)}, u32[]{:S(2)}, u32[]{:S(2)}) async-start(bf16[32,32,128]{2,1,0:T(8,128)(2,1)} %bitcast.59), calls=%async_computation.5 | async-start | bytes 524288 | tf_op jit(solution)/shard_map/all_to_all | solution.py:163
  12.5 18.1 %copy-start.3 = (bf16[128,4096]{1,0:T(8,128)(2,1)S(1)}, bf16[128,4096]{1,0:T(8,128)(2,1)}, u32[]{:S(2)}) copy-start(bf16[128,4096]{1,0:T(8,128)(2,1)} %param.8) | copy-start | bytes 3145732
  24.6 0.7 copy-start.6
  25.3 22.6 %all-to-all-start = ((bf16[32,64,128]{2,1,0:T(8,128)(2,1)}), bf16[32,64,128]{2,1,0:T(8,128)(2,1)}, u32[]{:S(2)}, u32[]{:S(2)}) async-start(bf16[32,64,128]{2,1,0:T(8,128)(2,1)} %pad_maximum_fusion.2), calls=%async_computation | async-start | bytes 1048576 | tf_op jit(solution)/shard_map/all_to_all | solution.py:163
  47.9 4.2 %copy-start.4 = (bf16[128,4096]{1,0:T(8,128)(2,1)S(1)}, bf16[128,4096]{1,0:T(8,128)(2,1)}, u32[]{:S(2)}) copy-start(bf16[128,4096]{1,0:T(8,128)(2,1)} %param.6) | copy-start | bytes 3145732
  47.9 55.9 %all-to-all-start.1 = ((bf16[32,256,128]{2,1,0:T(8,128)(2,1)}), bf16[32,256,128]{2,1,0:T(8,128)(2,1)S(1)}, u32[]{:S(2)}, u32[]{:S(2)}) async-start(bf16[32,256,128]{2,1,0:T(8,128)(2,1)} %bitcast.63), calls=%async_computation.1 | async-start | bytes 4194304 | tf_op jit(solution)/shard_map/all_to_all | solution.py:163
  103.8 5.2 %copy-start.1 = (bf16[32,256,128]{2,1,0:T(8,128)(2,1)}, bf16[32,256,128]{2,1,0:T(8,128)(2,1)S(1)}, u32[]{:S(2)}) copy-start(bf16[32,256,128]{2,1,0:T(8,128)(2,1)S(1)} %all-to-all-done.1.kv_ref) | copy-start | bytes 6291460
  103.8 29.4 %all-to-all-start.3 = ((bf16[32,64,128]{2,1,0:T(8,128)(2,1)}), bf16[32,64,128]{2,1,0:T(8,128)(2,1)S(1)}, u32[]{:S(2)}, u32[]{:S(2)}) async-start(bf16[32,64,128]{2,1,0:T(8,128)(2,1)} %bitcast_bitcast_fusion), calls=%async_computation.3 | async-start | bytes 1048576 | tf_op jit(solution)/shard_map/all_to_all | solution.py:163
  133.2 36.6 %copy-start.5 = (bf16[32,64,128]{2,1,0:T(8,128)(2,1)}, bf16[32,64,128]{2,1,0:T(8,128)(2,1)S(1)}, u32[]{:S(2)}) copy-start(bf16[32,64,128]{2,1,0:T(8,128)(2,1)S(1)} %all-to-all-done.3) | copy-start | bytes 1572868
  133.2 36.6 %all-to-all-start.6 = ((bf16[32,32,128]{2,1,0:T(8,128)(2,1)}), bf16[32,32,128]{2,1,0:T(8,128)(2,1)S(1)}, u32[]{:S(2)}, u32[]{:S(2)}) async-start(bf16[32,32,128]{2,1,0:T(8,128)(2,1)} %bitcast.71), calls=%async_computation.6 | async-start | bytes 524288 | tf_op jit(solution)/shard_map/all_to_all | solution.py:163
  169.7 36.3 %all-to-all-start.2 = ((bf16[32,64,128]{2,1,0:T(8,128)(2,1)}), bf16[32,64,128]{2,1,0:T(8,128)(2,1)S(1)}, u32[]{:S(2)}, u32[]{:S(2)}) async-start(bf16[32,64,128]{2,1,0:T(8,128)(2,1)} %bitcast.69), calls=%async_computation.2 | async-start | bytes 1048576 | tf_op jit(solution)/shard_map/all_to_all | solution.py:163
  206.0 26.3 %all-to-all-start.4 = ((bf16[32,64,128]{2,1,0:T(8,128)(2,1)}), bf16[32,64,128]{2,1,0:T(8,128)(2,1)S(1)}, u32[]{:S(2)}, u32[]{:S(2)}) async-start(bf16[32,64,128]{2,1,0:T(8,128)(2,1)} %bitcast.68), calls=%async_computation.4 | async-start | bytes 1048576 | tf_op jit(solution)/shard_map/all_to_all | solution.py:163

commit v2 on v1

--- a/solution.py
+++ b/solution.py
@@ -1,3 +1,4 @@
+import functools
 import math
 
 import jax
@@ -12,22 +13,21 @@
 SCALE = 0.125
 EXP2_SCALE = SCALE * math.log2(math.e)
 SUM_LOW, SUM_HIGH = 2.0**-60, 2.0**100
-QUERY_BLOCK = 512
+SOURCES_AT_ONCE = 8
 KEY_BLOCK = 4096
 SLOW_KEYS = 512
 VMEM_BYTES = 56 << 20
 CONTRACT_LAST = (((1,), (1,)), ((), ()))
 
 
-def prepare_kernel(length_ref, kv_ref, key_ref, value_ref):
+def prepare_kernel(rows, length_ref, kv_ref, key_ref, value_ref):
     length = length_ref[0]
     sources = kv_ref.shape[0]
-    rows = kv_ref.shape[1] // 2
     group = max(1, 512 // rows)
 
     def step(g, carry):
         keys = kv_ref[pl.ds(g * group, group), :rows, :].reshape(group * rows, LANES)
-        values = kv_ref[pl.ds(g * group, group), rows:, :].reshape(group * rows, LANES)
+        values = kv_ref[pl.ds(g * group, group), rows : 2 * rows, :].reshape(group * rows, LANES)
         start = pl.multiple_of(g * group * rows, group * rows)
         position = start + lax.broadcasted_iota(jnp.int32, (group * rows, LANES), 0)
         live = position < length
@@ -45,11 +45,11 @@
     lax.fori_loop(0, sources // group, step, 0)
 
 
-def prepare(valid_len, kv):
-    keys = kv.shape[0] * kv.shape[1] // 2
+def prepare(valid_len, kv, rows):
+    keys = kv.shape[0] * rows
     vmem = pl.BlockSpec(memory_space=pltpu.VMEM)
     return pl.pallas_call(
-        prepare_kernel,
+        functools.partial(prepare_kernel, rows),
         in_specs=[pl.BlockSpec(memory_space=pltpu.SMEM), vmem],
         out_specs=[vmem, vmem],
         out_shape=[
@@ -61,9 +61,12 @@
     )(valid_len, kv)
 
 
-def attend_kernel(query_ref, key_ref, value_ref, out_ref, score_ref):
+def attend_kernel(begin, query_ref, key_ref, value_ref, out_ref, score_ref):
     keys = key_ref.shape[0]
-    lane = lax.broadcasted_iota(jnp.int32, (QUERY_BLOCK, LANES), 1)
+    part = out_ref.shape[1]
+    group = SOURCES_AT_ONCE
+    block_rows = group * part
+    lane = lax.broadcasted_iota(jnp.int32, (block_rows, LANES), 1)
 
     def head_queries(queries):
         zeros = jnp.zeros_like(queries)
@@ -81,22 +84,23 @@
             preferred_element_type=jnp.float32,
         )
 
-    def store(rows, totals):
+    def store(sources, totals):
         mixed = jnp.concatenate([t[:DH] / t[DH : DH + 1] for t in totals], axis=0)
-        out_ref[rows, :] = mixed.T.astype(jnp.bfloat16)
+        out_ref[sources] = mixed.T.astype(jnp.bfloat16).reshape(group, part, LANES)
 
     def block(index, carry):
-        rows = pl.ds(pl.multiple_of(index * QUERY_BLOCK, QUERY_BLOCK), QUERY_BLOCK)
-        queries = head_queries(query_ref[rows, :])
+        sources = pl.ds(index * group, group)
+        block_queries = query_ref[sources, begin : begin + part, :]
+        queries = head_queries(block_queries.reshape(block_rows, LANES))
         totals = []
         for head in range(2):
             total = None
             for start in range(0, keys, KEY_BLOCK):
                 weights = jnp.exp2(scores(queries[head], start, KEY_BLOCK) * EXP2_SCALE)
-                part = weigh(head, weights, start, KEY_BLOCK)
-                total = part if total is None else total + part
+                found = weigh(head, weights, start, KEY_BLOCK)
+                total = found if total is None else total + found
             totals.append(total)
-        store(rows, totals)
+        store(sources, totals)
         sums = jnp.concatenate([t[DH : DH + 8] for t in totals], axis=0)
         safe = jnp.logical_and(sums >= SUM_LOW, sums <= SUM_HIGH)
         unsafe = jnp.max(jnp.where(safe, 0.0, 1.0)) > 0.0
@@ -113,7 +117,7 @@
                     return jnp.maximum(top, jnp.max(found, axis=0, keepdims=True))
 
                 top = lax.fori_loop(
-                    0, keys // SLOW_KEYS, first, jnp.full((1, QUERY_BLOCK), -jnp.inf, jnp.float32)
+                    0, keys // SLOW_KEYS, first, jnp.full((1, block_rows), -jnp.inf, jnp.float32)
                 )
 
                 def second(i, total):
@@ -123,32 +127,31 @@
 
                 totals.append(
                     lax.fori_loop(
-                        0, keys // SLOW_KEYS, second, jnp.zeros((DH + 16, QUERY_BLOCK), jnp.float32)
+                        0, keys // SLOW_KEYS, second, jnp.zeros((DH + 16, block_rows), jnp.float32)
                     )
                 )
-            store(rows, totals)
+            store(sources, totals)
 
         return carry
 
-    lax.fori_loop(0, query_ref.shape[0] // QUERY_BLOCK, block, 0)
-
-
-def attend(queries, keys, values):
-    sources, rows, _ = queries.shape
-    total, count = sources * rows, keys.shape[0]
+    lax.fori_loop(0, out_ref.shape[0] // group, block, 0)
+
+
+def attend(queries, begin, part, keys, values):
+    sources, count = queries.shape[0], keys.shape[0]
+    total = sources * part
     vmem = pl.BlockSpec(memory_space=pltpu.VMEM)
-    result = pl.pallas_call(
-        attend_kernel,
+    return pl.pallas_call(
+        functools.partial(attend_kernel, begin),
         in_specs=[vmem, vmem, vmem],
         out_specs=vmem,
-        out_shape=jax.ShapeDtypeStruct((total, LANES), jnp.bfloat16),
-        scratch_shapes=[pltpu.VMEM((count, QUERY_BLOCK), jnp.float32)],
+        out_shape=jax.ShapeDtypeStruct((sources, part, LANES), jnp.bfloat16),
+        scratch_shapes=[pltpu.VMEM((count, SOURCES_AT_ONCE * part), jnp.float32)],
         compiler_params=pltpu.CompilerParams(vmem_limit_bytes=VMEM_BYTES),
         cost_estimate=pl.CostEstimate(
             flops=total * count * 2 * 512 * 2, bytes_accessed=4 << 20, transcendentals=total * count * 2
         ),
-    )(queries.reshape(total, LANES), keys, values)
-    return result.reshape(sources, rows, LANES)
+    )(queries, keys, values)
 
 
 def by_owner(rows):
@@ -165,13 +168,18 @@
 
 def on_device(enc_query, enc_key, enc_value, dec_query, enc_length, tgt_length):
     rows_local = dec_query.shape[0]
-    kv = exchange(by_owner(jnp.concatenate([enc_key, enc_value], axis=0)))
-    cuts = (0, 32, 96, 128)
-    sent = [by_owner(enc_query[a:b]) for a, b in zip(cuts, cuts[1:])]
-    sent[0] = jnp.concatenate([by_owner(dec_query), sent[0]], axis=1)
-    arrived = [exchange(s) for s in sent]
-    keys, values = prepare(enc_length, kv)
-    returned = [exchange(attend(q, keys, values)) for q in arrived]
+    rows = enc_key.shape[0]
+    cut = 2 * rows_local
+    first = exchange(by_owner(jnp.concatenate([enc_key, enc_value, dec_query, enc_query[:cut]], axis=0)))
+    late, first = lax.optimization_barrier((by_owner(enc_query[cut:]), first))
+    late = exchange(late)
+    keys, values = prepare(enc_length, first, rows)
+    mixed = attend(first, 2 * rows, rows_local + cut, keys, values)
+    mixed, late = lax.optimization_barrier((mixed, late))
+    returned = [exchange(mixed)]
+    mixed = attend(late, 0, rows - cut, keys, values)
+    mixed, returned[0] = lax.optimization_barrier((mixed, returned[0]))
+    returned.append(exchange(mixed))
     returned_cross, returned[0] = returned[0][:, :rows_local], returned[0][:, rows_local:]
     enc_mixed = jnp.concatenate([by_row(r) for r in returned], axis=0)
     first_row = lax.axis_index("seq") * rows_local

time: 234 us -> 195 us (0.83)
  starting transfers between devices: 47.4 us -> 30.3 us
  Pallas kernels: 80.4 us -> 70.8 us
  waiting for transfers between devices: 90.8 us -> 83.5 us
  local copies, waits for them, and re-layouts: 8.65 us -> 2.32 us
    all_to_all x7 -> x4, starting transfers between devices: 47.4 us -> 30.3 us  [exchange(): lax.all_to_all(blocks, 'seq', split_axis=0, concat_axis=0, tiled=True)]
    pallas_call x4 -> x3, Pallas kernels: 80.4 us -> 70.8 us  [the longest x2 66.5 us: attend(): pl.pallas_call(functools.partial(attend_kernel, begin), in_specs=[vmem, v...]
    all_to_all x7 -> x4, waiting for transfers between devices: 90.8 us -> 83.5 us  [exchange(): lax.all_to_all(blocks, 'seq', split_axis=0, concat_axis=0, tiled=True)]
    unnamed x18 -> x4, local copies, waits for them, and re-layouts: 3.85 us -> 0.01 us
    transpose x0 -> x1, other arithmetic: none -> 3.12 us  [by_owner(): return rows.reshape(rows.shape[0], -1, LANES).transpose(1, 0, 2)]
    reshape x3 -> x1, local copies, waits for them, and re-layouts: 3.68 us -> 0.94 us  [by_owner(): return rows.reshape(rows.shape[0], -1, LANES).transpose(1, 0, 2)]
  transfers between devices with their start and end apart: 7 -> 4, of which waited for: 4 -> 2; matrix products, arithmetic and copies ran while one was open for 4% -> 1% of each run, Pallas kernels for 34% -> 36%
where the time goes in v2:
time: 195 us; the launch traced here: 194 us
  waiting for transfers between devices  83.5 us (43%)
  Pallas kernels  70.8 us (36%)
  starting transfers between devices  30.3 us (16%)
  other arithmetic  5.01 us (3%)
  local copies, waits for them, and re-layouts  2.32 us (1%)
  between operations  2.01 us (1%)
    all_to_all x4, waiting for transfers between devices, exchange(): lax.all_to_all(blocks, 'seq', split_axis=0, concat_axis=0, tiled=True)  83.5 us
    pallas_call x2, Pallas kernels, attend(): pl.pallas_call(functools.partial(attend_kernel, begin), in_specs=[vmem, v...  66.5 us
    all_to_all x4, starting transfers between devices, exchange(): lax.all_to_all(blocks, 'seq', split_axis=0, concat_axis=0, tiled=True)  30.3 us
    pallas_call x1, Pallas kernels, prepare(): pl.pallas_call(functools.partial(prepare_kernel, rows), in_specs=[pl.Bloc...  4.23 us
  transfers between devices with their start and end apart: 4, of which 2 were waited for; matrix products, arithmetic and copies ran while one was open for 1% of the time, Pallas kernels for 36%

profile of v2, /device:TPU:2, one launch (start us, length us, event | category | flops | bytes accessed | tf_op | source)
XLA Modules:
  0.0 193.9 jit_solution(10838127074301365083)
XLA Ops:
  0.6 1.3 fusion
  1.9 3.1 %bitcast_bitcast_fusion = bf16[32,352,128]{2,1,0:T(8,128)(2,1)} fusion(bf16[64,4096]{1,0:T(8,128)(2,1)S(1)} %get-tuple-element.18, bf16[32,4096]{1,0:T(8,128)(2,1)} %param.9, bf16[128,4096]{1,0:T(8,128)(2,1)} %param.8, bf16[128,4096]{1,0:T(8,128)(2,1)} %param.7), kind=kLoop, calls=%fused_computation | loop fusion | flops 11534336 | bytes 5767168 | tf_op jit(solution)/shard_map/transpose | solution.py:158
  5.0 9.9 %all-to-all-start = ((bf16[32,352,128]{2,1,0:T(8,128)(2,1)}), bf16[32,352,128]{2,1,0:T(8,128)(2,1)S(1)}, u32[]{:S(2)}, u32[]{:S(2)}) async-start(bf16[32,352,128]{2,1,0:T(8,128)(2,1)} %bitcast_bitcast_fusion), calls=%async_computation | async-start | bytes 5767168 | tf_op jit(solution)/shard_map/all_to_all | solution.py:166
  14.9 0.9 copy.23
  17.2 66.4 %all-to-all-done.kv_ref.query_ref = bf16[32,352,128]{2,1,0:T(8,128)(2,1)S(1)} async-done(((bf16[32,352,128]{2,1,0:T(8,128)(2,1)}), bf16[32,352,128]{2,1,0:T(8,128)(2,1)S(1)}, u32[]{:S(2)}, u32[]{:S(2)}) %all-to-all-start) | async-done | bytes 2883616 | tf_op jit(solution)/shard_map/all_to_all | solution.py:166
  83.5 0.0 copy-start
  83.5 3.9 %all-to-all-start.1 = ((bf16[32,64,128]{2,1,0:T(8,128)(2,1)}), bf16[32,64,128]{2,1,0:T(8,128)(2,1)S(1)}, u32[]{:S(2)}, u32[]{:S(2)}) async-start(bf16[32,64,128]{2,1,0:T(8,128)(2,1)} %bitcast.33), calls=%async_computation.1 | async-start | bytes 1048576 | tf_op jit(solution)/shard_map/all_to_all | solution.py:166
  87.4 0.0 copy-done
  87.4 4.2 %shard_map.77 = (bf16[4096,128]{1,0:T(8,128)(2,1)}, bf16[2,80,4096]{2,1,0:T(8,128)(2,1)}) custom-call(s32[1]{0:T(128)S(6)} %copy.24.length_ref, bf16[32,352,128]{2,1,0:T(8,128)(2,1)} %copy-done), custom_call_target="tpu_custom_call" | custom-call | bytes 6291456 | tf_op jit(solution)/shard_map/pallas_call | solution.py:51
  91.7 38.4 %shard_map.78 = bf16[32,96,128]{2,1,0:T(8,128)(2,1)} custom-call(bf16[32,352,128]{2,1,0:T(8,128)(2,1)} %copy-done, bf16[4096,128]{1,0:T(8,128)(2,1)} %get-tuple-element.11.key_ref, bf16[2,80,4096]{2,1,0:T(8,128)(2,1)} %get-tuple-element.12.value_ref), custom_call_target="tpu_custom_call" | custom-call | flops 25769803776 | bytes 4194304 | tf_op jit(solution)/shard_map/pallas_call | solution.py:144
  130.1 0.0 all-to-all-done.1.query_ref
  130.1 0.0 copy-start.1
  130.1 8.4 %all-to-all-start.2 = ((bf16[32,96,128]{2,1,0:T(8,128)(2,1)}), bf16[32,96,128]{2,1,0:T(8,128)(2,1)S(1)}, u32[]{:S(2)}, u32[]{:S(2)}) async-start(bf16[32,96,128]{2,1,0:T(8,128)(2,1)} %shard_map.78), calls=%async_computation.2 | async-start | bytes 1572864 | tf_op jit(solution)/shard_map/all_to_all | solution.py:166
  138.5 0.0 copy-done.1
  138.5 28.1 %shard_map.79 = bf16[32,64,128]{2,1,0:T(8,128)(2,1)} custom-call(bf16[32,64,128]{2,1,0:T(8,128)(2,1)} %copy-done.1, bf16[4096,128]{1,0:T(8,128)(2,1)} %get-tuple-element.11.key_ref, bf16[2,80,4096]{2,1,0:T(8,128)(2,1)} %get-tuple-element.12.value_ref), custom_call_target="tpu_custom_call" | custom-call | flops 17179869184 | bytes 4194304 | tf_op jit(solution)/shard_map/pallas_call | solution.py:144
  166.6 0.0 all-to-all-done.2
  166.6 8.1 %all-to-all-start.3 = ((bf16[32,64,128]{2,1,0:T(8,128)(2,1)}), bf16[32,64,128]{2,1,0:T(8,128)(2,1)S(1)}, u32[]{:S(2)}, u32[]{:S(2)}) async-start(bf16[32,64,128]{2,1,0:T(8,128)(2,1)} %shard_map.79), calls=%async_computation.3 | async-start | bytes 1048576 | tf_op jit(solution)/shard_map/all_to_all | solution.py:166
  174.8 0.8 bitcast_select_fusion
  175.6 17.2 %all-to-all-done.3 = bf16[32,64,128]{2,1,0:T(8,128)(2,1)S(1)} async-done(((bf16[32,64,128]{2,1,0:T(8,128)(2,1)}), bf16[32,64,128]{2,1,0:T(8,128)(2,1)S(1)}, u32[]{:S(2)}, u32[]{:S(2)}) %all-to-all-start.3) | async-done | bytes 524320 | tf_op jit(solution)/shard_map/all_to_all | solution.py:166
  192.8 0.1 copy_bitcast_fusion
  192.9 1.1 pad_maximum_fusion
  (2 shorter events, 0.0 us)
Async XLA Ops:
  5.0 78.5 %all-to-all-start = ((bf16[32,352,128]{2,1,0:T(8,128)(2,1)}), bf16[32,352,128]{2,1,0:T(8,128)(2,1)S(1)}, u32[]{:S(2)}, u32[]{:S(2)}) async-start(bf16[32,352,128]{2,1,0:T(8,128)(2,1)} %bitcast_bitcast_fusion), calls=%async_computation | async-start | bytes 5767168 | tf_op jit(solution)/shard_map/all_to_all | solution.py:166
  83.5 3.9 %copy-start = (bf16[32,352,128]{2,1,0:T(8,128)(2,1)}, bf16[32,352,128]{2,1,0:T(8,128)(2,1)S(1)}, u32[]{:S(2)}) copy-start(bf16[32,352,128]{2,1,0:T(8,128)(2,1)S(1)} %all-to-all-done.kv_ref.query_ref) | copy-start | bytes 8650756
  83.5 46.6 %all-to-all-start.1 = ((bf16[32,64,128]{2,1,0:T(8,128)(2,1)}), bf16[32,64,128]{2,1,0:T(8,128)(2,1)S(1)}, u32[]{:S(2)}, u32[]{:S(2)}) async-start(bf16[32,64,128]{2,1,0:T(8,128)(2,1)} %bitcast.33), calls=%async_computation.1 | async-start | bytes 1048576 | tf_op jit(solution)/shard_map/all_to_all | solution.py:166
  130.1 8.4 %copy-start.1 = (bf16[32,64,128]{2,1,0:T(8,128)(2,1)}, bf16[32,64,128]{2,1,0:T(8,128)(2,1)S(1)}, u32[]{:S(2)}) copy-start(bf16[32,64,128]{2,1,0:T(8,128)(2,1)S(1)} %all-to-all-done.1.query_ref) | copy-start | bytes 1572868
  130.1 36.6 %all-to-all-start.2 = ((bf16[32,96,128]{2,1,0:T(8,128)(2,1)}), bf16[32,96,128]{2,1,0:T(8,128)(2,1)S(1)}, u32[]{:S(2)}, u32[]{:S(2)}) async-start(bf16[32,96,128]{2,1,0:T(8,128)(2,1)} %shard_map.78), calls=%async_computation.2 | async-start | bytes 1572864 | tf_op jit(solution)/shard_map/all_to_all | solution.py:166
  166.6 26.1 %all-to-all-start.3 = ((bf16[32,64,128]{2,1,0:T(8,128)(2,1)}), bf16[32,64,128]{2,1,0:T(8,128)(2,1)S(1)}, u32[]{:S(2)}, u32[]{:S(2)}) async-start(bf16[32,64,128]{2,1,0:T(8,128)(2,1)} %shard_map.79), calls=%async_computation.3 | async-start | bytes 1048576 | tf_op jit(solution)/shard_map/all_to_all | solution.py:166

commit v3 on v0

v3 whole, which is shorter than its diff:
```python
import functools
import math

import jax
import jax.numpy as jnp
from jax import lax
from jax.experimental import pallas as pl
from jax.experimental.pallas import tpu as pltpu
from jax.sharding import PartitionSpec as P

DH = 64
LANES = 128
SCALE = 0.125
EXP2_SCALE = SCALE * math.log2(math.e)
SUM_LOW, SUM_HIGH = 2.0**-60, 2.0**100
SOURCES_AT_ONCE = 8
SLOW_KEYS = 512
VMEM_BYTES = 56 << 20
SMEM = pl.BlockSpec(memory_space=pltpu.SMEM)
VMEM = pl.BlockSpec(memory_space=pltpu.VMEM)
HBM = pl.BlockSpec(memory_space=pl.ANY)
CONTRACT_FIRST = (((0,), (0,)), ((), ()))
CONTRACT_LAST = (((1,), (1,)), ((), ()))


def prepare(length, rows, offset, stride, block_ref, copies, key_ref, value_ref):
    group = block_ref.shape[0] // len(copies)
    count = group * rows
    for g, copy in enumerate(copies):
        copy.wait()
        sources = slice(g * group, (g + 1) * group)
        keys = block_ref[sources, :rows, :].reshape(count, LANES)
        values = block_ref[sources, rows : 2 * rows, :].reshape(count, LANES)

        def live(axis, shape):
            i = lax.broadcasted_iota(jnp.int32, shape, axis)
            return i + lax.div(i, rows) * (stride - rows) + (g * group * stride + offset) < length

        here = slice(g * count, (g + 1) * count)
        kept = live(0, (count, LANES))
        zeros = jnp.zeros_like(keys)
        key_ref[here, :] = jnp.where(kept, keys, zeros)
        flipped = jnp.where(kept, values, zeros).T
        ones = jnp.where(live(1, (16, count)), 1.0, 0.0).astype(jnp.bfloat16)
        for head in range(2):
            value_ref[head, :DH, here] = flipped[head * DH : (head + 1) * DH]
            value_ref[head, DH:, here] = ones


def at_once(rows):
    return 512 // rows if 512 % rows == 0 else 4


def arrive(source, block, sems, rows):
    group = at_once(rows)
    copies = []
    for g in range(block.shape[0] // group):
        here = pl.ds(g * group, group)
        copies.append(pltpu.make_async_copy(source.at[here], block.at[here], sems.at[g]))
        copies[-1].start()
    return copies


def scores(key_ref, queries, start, count):
    return lax.dot_general(
        key_ref[pl.ds(start, count), :], queries, CONTRACT_LAST, preferred_element_type=jnp.float32
    )


def weigh(value_ref, head, weights, start, count):
    return jnp.dot(
        value_ref[head, :, pl.ds(start, count)], weights.astype(jnp.bfloat16), preferred_element_type=jnp.float32
    )


def quick(head, queries, key_ref, value_ref):
    keys = key_ref.shape[0]
    weights = jnp.exp2(scores(key_ref, queries, 0, keys) * EXP2_SCALE)
    return weigh(value_ref, head, weights, 0, keys)


def head_queries(query_ref, sources, begin, part):
    block_rows = SOURCES_AT_ONCE * part
    queries = query_ref[sources, begin : begin + part, :].reshape(block_rows, LANES)
    lane = lax.broadcasted_iota(jnp.int32, (block_rows, LANES), 1)
    zeros = jnp.zeros_like(queries)
    return [jnp.where(lane < DH, queries, zeros), jnp.where(lane < DH, zeros, queries)]


def begin_rows(begin, part, query_ref, key_ref, value_ref, total_ref):
    def block(index, carry):
        queries = head_queries(query_ref, pl.ds(index * SOURCES_AT_ONCE, SOURCES_AT_ONCE), begin, part)
        for head in range(2):
            total_ref[index, head] = quick(head, queries[head], key_ref, value_ref)
        return carry

    lax.fori_loop(0, total_ref.shape[0], block, 0)


def finish_rows(begin, part, query_ref, parts, total_ref, out_ref, fetch_first=None):
    block_rows = SOURCES_AT_ONCE * part

    def block(index, carry):
        sources = pl.ds(index * SOURCES_AT_ONCE, SOURCES_AT_ONCE)
        queries = head_queries(query_ref, sources, begin, part)

        def store(totals):
            mixed = jnp.concatenate([t[:DH] / t[DH : DH + 1] for t in totals], axis=0)
            out_ref[sources] = mixed.T.astype(jnp.bfloat16).reshape(SOURCES_AT_ONCE, part, LANES)

        totals = []
        for head in range(2):
            total = quick(head, queries[head], *parts[0]) if total_ref is None else total_ref[index, head]
            totals.append(total + quick(head, queries[head], *parts[1]))
        store(totals)
        sums = jnp.concatenate([t[DH : DH + 8] for t in totals], axis=0)
        safe = jnp.logical_and(sums >= SUM_LOW, sums <= SUM_HIGH)
        unsafe = jnp.max(jnp.where(safe, 0.0, 1.0)) > 0.0

        @pl.when(unsafe)
        def _():
            if fetch_first is not None:
                fetch_first()
            pick = lax.broadcasted_iota(jnp.int32, (16, block_rows), 0) == 0
            pick = jnp.where(pick, 1.0, 0.0).astype(jnp.bfloat16)
            totals = []
            for head in range(2):

                def found(key_ref, value_ref, start, head=head):
                    live = lax.dot_general(
                        value_ref[head, DH:, pl.ds(start, SLOW_KEYS)],
                        pick,
                        CONTRACT_FIRST,
                        preferred_element_type=jnp.float32,
                    )
                    return jnp.where(live > 0.5, scores(key_ref, queries[head], start, SLOW_KEYS), -jnp.inf)

                top = jnp.full((1, block_rows), -jnp.inf, jnp.float32)
                total = jnp.zeros((DH + 16, block_rows), jnp.float32)
                for key_ref, value_ref in parts:

                    def first(i, top, key_ref=key_ref, value_ref=value_ref):
                        start = pl.multiple_of(i * SLOW_KEYS, SLOW_KEYS)
                        return jnp.maximum(top, jnp.max(found(key_ref, value_ref, start), axis=0, keepdims=True))

                    top = lax.fori_loop(0, key_ref.shape[0] // SLOW_KEYS, first, top)
                for key_ref, value_ref in parts:

                    def second(i, total, key_ref=key_ref, value_ref=value_ref, head=head, top=top):
                        start = pl.multiple_of(i * SLOW_KEYS, SLOW_KEYS)
                        weights = jnp.exp2((found(key_ref, value_ref, start) - top) * EXP2_SCALE)
                        return total + weigh(value_ref, head, weights, start, SLOW_KEYS)

                    total = lax.fori_loop(0, key_ref.shape[0] // SLOW_KEYS, second, total)
                totals.append(total)
            store(totals)

        return carry

    lax.fori_loop(0, out_ref.shape[0] // SOURCES_AT_ONCE, block, 0)


def begin_kernel(shape, part, length_ref, arrived, total_ref, keys_out, values_out, *scratch):
    rows, offset, stride = shape
    block, key_ref, value_ref, sems, out_sems = scratch
    prepare(length_ref[0], rows, offset, stride, block, arrive(arrived, block, sems, rows), key_ref, value_ref)
    kept = [
        pltpu.make_async_copy(key_ref, keys_out, out_sems.at[0]),
        pltpu.make_async_copy(value_ref, values_out, out_sems.at[1]),
    ]
    for copy in kept:
        copy.start()
    begin_rows(2 * rows, part, block, key_ref, value_ref, total_ref)
    for copy in kept:
        copy.wait()


def finish_first_kernel(shape, begin, part, length_ref, arrived, queries, *refs):
    rows, offset, stride = shape
    early_keys, early_values, total, out_ref, keys_out, values_out = refs[:6]
    block, query_block, key_ref, value_ref, early_key_ref, early_value_ref, total_ref = refs[6:13]
    sems, out_sems = refs[13:]
    arrivals = arrive(arrived, block, sems, rows)
    fetches = [
        pltpu.make_async_copy(queries.at[:, pl.ds(begin, part), :], query_block, out_sems.at[2]),
        pltpu.make_async_copy(total, total_ref, out_sems.at[3]),
    ]
    for fetch in fetches:
        fetch.start()
    prepare(length_ref[0], rows, offset, stride, block, arrivals, key_ref, value_ref)
    kept = [
        pltpu.make_async_copy(key_ref, keys_out, out_sems.at[0]),
        pltpu.make_async_copy(value_ref, values_out, out_sems.at[1]),
    ]
    for copy in kept:
        copy.start()
    for fetch in fetches:
        fetch.wait()

    def fetch_first():
        copies = [
            pltpu.make_async_copy(early_keys, early_key_ref, out_sems.at[4]),
            pltpu.make_async_copy(early_values, early_value_ref, out_sems.at[5]),
        ]
        for copy in copies:
            copy.start()
        for copy in copies:
            copy.wait()

    parts = [(early_key_ref, early_value_ref), (key_ref, value_ref)]
    finish_rows(0, part, query_block, parts, total_ref, out_ref, fetch_first)
    for copy in kept:
        copy.wait()


def finish_second_kernel(begin, part, queries, early_keys, early_values, keys, values, out_ref, query_block, sem):
    fetch = pltpu.make_async_copy(queries.at[:, pl.ds(begin, part), :], query_block, sem)
    fetch.start()
    fetch.wait()
    finish_rows(0, part, query_block, [(early_keys, early_values), (keys, values)], None, out_ref)


def call(kernel, in_specs, out_specs, out_shape, args, work, scratch):
    return pl.pallas_call(
        kernel,
        in_specs=in_specs,
        out_specs=out_specs,
        out_shape=out_shape,
        scratch_shapes=scratch,
        compiler_params=pltpu.CompilerParams(vmem_limit_bytes=VMEM_BYTES),
        cost_estimate=pl.CostEstimate(flops=work * 2 * 512 * 2, bytes_accessed=8 << 20, transcendentals=work * 2),
    )(*args)


def bf16(*shape):
    return jax.ShapeDtypeStruct(shape, jnp.bfloat16)


def attend(valid_len, first, second, rows_first, rows_second):
    sources = first.shape[0]
    stride = rows_first + rows_second
    begins = 2 * rows_first, 2 * rows_second
    parts = first.shape[1] - begins[0], second.shape[1] - begins[1]
    groups = sources // SOURCES_AT_ONCE

    def kept(rows):
        shapes = [bf16(sources * rows, LANES), bf16(2, DH + 16, sources * rows)]
        scratch = [pltpu.VMEM(x.shape, x.dtype) for x in shapes]
        return shapes, scratch, pltpu.SemaphoreType.DMA((sources // at_once(rows),))

    def work(part, rows):
        return sources * part * sources * rows

    shapes, early_scratch, arrivals = kept(rows_first)
    total, *early = call(
        functools.partial(begin_kernel, (rows_first, 0, stride), parts[0]),
        [SMEM, HBM],
        [VMEM, HBM, HBM],
        [jax.ShapeDtypeStruct((groups, 2, DH + 16, SOURCES_AT_ONCE * parts[0]), jnp.float32)] + shapes,
        (valid_len, first),
        work(parts[0], rows_first),
        [pltpu.VMEM(first.shape, first.dtype), *early_scratch, arrivals, pltpu.SemaphoreType.DMA((2,))],
    )
    query_blocks = [pltpu.VMEM((sources, part, LANES), jnp.bfloat16) for part in parts]
    shapes, scratch, arrivals = kept(rows_second)
    mixed, *late = call(
        functools.partial(finish_first_kernel, (rows_second, rows_first, stride), begins[0], parts[0]),
        [SMEM] + [HBM] * 5,
        [VMEM, HBM, HBM],
        [bf16(sources, parts[0], LANES)] + shapes,
        (valid_len, second, first, *early, total),
        work(parts[0], rows_second),
        [
            pltpu.VMEM(second.shape, second.dtype),
            query_blocks[0],
            *scratch,
            *early_scratch,
            pltpu.VMEM(total.shape, total.dtype),
            arrivals,
            pltpu.SemaphoreType.DMA((6,)),
        ],
    )
    yield mixed
    yield call(
        functools.partial(finish_second_kernel, begins[1], parts[1]),
        [HBM] + [VMEM] * 4,
        VMEM,
        bf16(sources, parts[1], LANES),
        (second, *early, *late),
        work(parts[1], stride),
        [query_blocks[1], pltpu.SemaphoreType.DMA],
    )


def by_owner(rows):
    return rows.reshape(rows.shape[0], -1, LANES).transpose(1, 0, 2)


def by_row(blocks):
    return blocks.transpose(1, 0, 2).reshape(blocks.shape[1], -1)


def exchange(blocks):
    return lax.all_to_all(blocks, "seq", split_axis=0, concat_axis=0, tiled=True)


def on_device(enc_query, enc_key, enc_value, dec_query, enc_length, tgt_length):
    rows_local = dec_query.shape[0]
    rows = enc_key.shape[0]
    cut, query_cut = rows - rows_local, 2 * rows_local
    first = [enc_key[:cut], enc_value[:cut], dec_query, enc_query[:query_cut]]
    first = exchange(by_owner(jnp.concatenate(first, axis=0)))
    second = [enc_key[cut:], enc_value[cut:], enc_query[query_cut:]]
    second, first = lax.optimization_barrier((by_owner(jnp.concatenate(second, axis=0)), first))
    second = exchange(second)
    returned = []
    for mixed in attend(enc_length, first, second, cut, rows - cut):
        if returned:
            mixed, returned[-1] = lax.optimization_barrier((mixed, returned[-1]))
        returned.append(exchange(mixed))
    returned_cross, returned[0] = returned[0][:, :rows_local], returned[0][:, rows_local:]
    enc_mixed = jnp.concatenate([by_row(r) for r in returned], axis=0)
    first_row = lax.axis_index("seq") * rows_local
    keep_rows = first_row + jnp.arange(rows_local, dtype=jnp.int32) < tgt_length[0]
    crossed = by_row(returned_cross)
    cross_mixed = jnp.where(keep_rows[:, None], crossed, jnp.zeros_like(crossed))
    return (enc_mixed, cross_mixed)


def solution(mesh):
    return jax.shard_map(
        on_device,
        mesh=mesh,
        in_specs=(
            P(("dp", "seq"), None),
            P(("dp", "seq"), None),
            P(("dp", "seq"), None),
            P(("dp", "seq"), None),
            P("dp"),
            P("dp"),
        ),
        out_specs=(P(("dp", "seq"), None), P(("dp", "seq"), None)),
        check_vma=False,
    )
```

time: 373 us -> 201 us (0.54)
  matrix products: 184 us -> 0 us
  Pallas kernels: 0 us -> 84.9 us
  waiting for transfers between devices: 116 us -> 74.2 us
  local copies, waits for them, and re-layouts: 27.4 us -> 6.94 us
  starting transfers between devices: 34.5 us -> 27.1 us
    sub x10 -> x0, matrix products: 99.2 us -> none  [one_block(): weights = jnp.exp(scores - row_max)]
    dot_general x10 -> x0, matrix products: 84.9 us -> none  [one_block(): jnp.einsum('hbk,khd->bhd', weights, value_heads, preferred_element_type=j...]
    pallas_call x0 -> x3, Pallas kernels: none -> 84.9 us  [call(): pl.pallas_call(kernel, in_specs=in_specs, out_specs=out_specs, out_shape=...]
    all_to_all x6 -> x4, waiting for transfers between devices: 116 us -> 74.2 us  [exchange(): lax.all_to_all(blocks, 'seq', split_axis=0, concat_axis=0, tiled=True)]
    all_to_all x6 -> x4, starting transfers between devices: 34.5 us -> 27.1 us  [exchange(): lax.all_to_all(blocks, 'seq', split_axis=0, concat_axis=0, tiled=True)]
    lt x10 -> x0, other arithmetic: 7.1 us -> none  [attend_block(): live_keys = jnp.arange(key_rows, dtype=jnp.int32) < valid_len]
    dynamic_update_slice x20 -> x0, local copies, waits for them, and re-layouts: 6.65 us -> none  [attend_block(): lax.map(one_block, queries.reshape(blocks_num, row_block, col_width))]
    unnamed x6 -> x7, local copies, waits for them, and re-layouts: 8.14 us -> 2.45 us
  transfers between devices with their start and end apart: 6 -> 4, of which waited for: 5 -> 3; matrix products, arithmetic and copies ran while one was open for 47% -> 3% of each run, Pallas kernels for 0% -> 28%
where the time goes in v3:
time: 201 us
  Pallas kernels  84.9 us (42%)
  waiting for transfers between devices  74.2 us (37%)
  starting transfers between devices  27.1 us (13%)
  local copies, waits for them, and re-layouts  6.94 us (3%)
  other arithmetic  5.44 us (3%)
  between operations  2.08 us (1%)
    pallas_call x3, Pallas kernels, call(): pl.pallas_call(kernel, in_specs=in_specs, out_specs=out_specs, out_shape=...  84.9 us
    all_to_all x4, waiting for transfers between devices, exchange(): lax.all_to_all(blocks, 'seq', split_axis=0, concat_axis=0, tiled=True)  74.2 us
    all_to_all x4, starting transfers between devices, exchange(): lax.all_to_all(blocks, 'seq', split_axis=0, concat_axis=0, tiled=True)  27.1 us
  transfers between devices with their start and end apart: 4, of which 3 were waited for; matrix products, arithmetic and copies ran while one was open for 3% of the time, Pallas kernels for 28%

profile of v3, /device:TPU:2, one launch (start us, length us, event | category | flops | bytes accessed | tf_op | source)
XLA Modules:
  0.0 200.7 jit_solution(6873956268705096765)
XLA Ops:
  0.6 0.0 slice-start
  0.6 0.0 slice-start.2
  0.7 0.0 copy-start.1
  0.7 1.4 fusion
  2.1 0.0 slice-done
  2.1 0.2 slice-done.2
  2.3 0.0 copy-done.1
  2.4 1.6 bitcast_bitcast_fusion
  4.0 10.0 %all-to-all-start = ((bf16[32,288,128]{2,1,0:T(8,128)(2,1)}), bf16[32,288,128]{2,1,0:T(8,128)(2,1)}, u32[]{:S(2)}, u32[]{:S(2)}) async-start(bf16[32,288,128]{2,1,0:T(8,128)(2,1)} %bitcast_bitcast_fusion), calls=%async_computation | async-start | bytes 4718592 | tf_op jit(solution)/shard_map/all_to_all | solution.py:304
  14.0 0.0 slice-start.1
  14.0 0.0 slice-start.3
  14.0 0.5 copy.18
  14.5 0.4 slice-done.1
  14.9 0.5 copy.16
  15.4 0.0 slice-done.3
  15.4 0.5 copy.17
  15.9 1.9 pad_maximum_fusion
  17.8 2.3 %copy.11 = bf16[128,32,128]{2,0,1:T(8,128)(2,1)} copy(bf16[128,32,128]{0,2,1:T(8,128)(2,1)} %bitcast.29) | data formatting | bytes 2097152 | tf_op jit(solution)/shard_map/reshape | solution.py:296
  20.1 49.6 %all-to-all-done.arrived.queries = bf16[32,288,128]{2,1,0:T(8,128)(2,1)} async-done(((bf16[32,288,128]{2,1,0:T(8,128)(2,1)}), bf16[32,288,128]{2,1,0:T(8,128)(2,1)}, u32[]{:S(2)}, u32[]{:S(2)}) %all-to-all-start) | async-done | bytes 2359328 | tf_op jit(solution)/shard_map/all_to_all | solution.py:304
  69.7 5.0 %all-to-all-start.1 = ((bf16[32,128,128]{2,1,0:T(8,128)(2,1)}), bf16[32,128,128]{2,1,0:T(8,128)(2,1)S(1)}, u32[]{:S(2)}, u32[]{:S(2)}) async-start(bf16[32,128,128]{2,1,0:T(8,128)(2,1)} %bitcast.1), calls=%async_computation.1 | async-start | bytes 2097152 | tf_op jit(solution)/shard_map/all_to_all | solution.py:304
  76.0 20.2 %shard_map.77 = (f32[4,2,80,768]{3,2,1,0:T(8,128)}, bf16[3072,128]{1,0:T(8,128)(2,1)}, bf16[2,80,3072]{2,1,0:T(8,128)(2,1)}) custom-call(s32[1]{0:T(128)S(6)} %copy.27.length_ref, bf16[32,288,128]{2,1,0:T(8,128)(2,1)} %all-to-all-done.arrived.queries), custom_call_target="tpu_custom_call" | custom-call | flops 19327352832 | bytes 8388608 | tf_op jit(solution)/shard_map/pallas_call | solution.py:224
  96.2 7.4 %all-to-all-done.1.arrived.queries = bf16[32,128,128]{2,1,0:T(8,128)(2,1)S(1)} async-done(((bf16[32,128,128]{2,1,0:T(8,128)(2,1)}), bf16[32,128,128]{2,1,0:T(8,128)(2,1)S(1)}, u32[]{:S(2)}, u32[]{:S(2)}) %all-to-all-start.1) | async-done | bytes 1048608 | tf_op jit(solution)/shard_map/all_to_all | solution.py:304
  103.6 0.0 copy-start
  103.6 1.0 copy-done
  104.6 29.4 %shard_map.78 = (bf16[32,96,128]{2,1,0:T(8,128)(2,1)}, bf16[1024,128]{1,0:T(8,128)(2,1)}, bf16[2,80,1024]{2,1,0:T(8,128)(2,1)}) custom-call(s32[1]{0:T(128)S(6)} %copy.27.length_ref, bf16[32,128,128]{2,1,0:T(8,128)(2,1)} %copy-done, bf16[32,288,128]{2,1,0:T(8,128)(2,1)} %all-to-all-done.arrived.queries, ...), custom_call_target="tpu_custom_call" | custom-call | flops 6442450944 | bytes 8388608 | tf_op jit(solution)/shard_map/pallas_call | solution.py:224
  134.0 4.1 %all-to-all-start.2 = ((bf16[32,96,128]{2,1,0:T(8,128)(2,1)}), bf16[32,96,128]{2,1,0:T(8,128)(2,1)S(1)}, u32[]{:S(2)}, u32[]{:S(2)}) async-start(bf16[32,96,128]{2,1,0:T(8,128)(2,1)} %get-tuple-element.19), calls=%async_computation.2 | async-start | bytes 1572864 | tf_op jit(solution)/shard_map/all_to_all | solution.py:304
  138.1 35.3 %shard_map.79 = bf16[32,64,128]{2,1,0:T(8,128)(2,1)} custom-call(bf16[32,128,128]{2,1,0:T(8,128)(2,1)} %copy-done, bf16[3072,128]{1,0:T(8,128)(2,1)} %get-tuple-element.14.refs_0_.early_keys, bf16[2,80,3072]{2,1,0:T(8,128)(2,1)} %get-tuple-element.15.refs_1_.early_values, bf16[1024,128]{1,0:T(8,128)(2,1)} %get-tuple-element.17.keys, ...), custom_call_target="tpu_custom_call" | custom-call | flops 17179869184 | bytes 8388608 | tf_op jit(solution)/shard_map/pallas_call | solution.py:224
  173.4 0.0 all-to-all-done.2
  173.5 8.1 %all-to-all-start.3 = ((bf16[32,64,128]{2,1,0:T(8,128)(2,1)}), bf16[32,64,128]{2,1,0:T(8,128)(2,1)S(1)}, u32[]{:S(2)}, u32[]{:S(2)}) async-start(bf16[32,64,128]{2,1,0:T(8,128)(2,1)} %shard_map.79), calls=%async_computation.3 | async-start | bytes 1048576 | tf_op jit(solution)/shard_map/all_to_all | solution.py:304
  181.5 0.8 bitcast_select_fusion
  182.4 17.2 %all-to-all-done.3 = bf16[32,64,128]{2,1,0:T(8,128)(2,1)S(1)} async-done(((bf16[32,64,128]{2,1,0:T(8,128)(2,1)}), bf16[32,64,128]{2,1,0:T(8,128)(2,1)S(1)}, u32[]{:S(2)}, u32[]{:S(2)}) %all-to-all-start.3) | async-done | bytes 524320 | tf_op jit(solution)/shard_map/all_to_all | solution.py:304
  199.6 0.1 copy_bitcast_fusion
  199.6 1.1 pad_maximum_fusion.1
  (2 shorter events, 0.0 us)
Async XLA Ops:
  0.6 1.5 slice-start
  0.6 1.7 slice-start.2
  0.7 1.7 copy-start.1
  4.0 65.7 %all-to-all-start = ((bf16[32,288,128]{2,1,0:T(8,128)(2,1)}), bf16[32,288,128]{2,1,0:T(8,128)(2,1)}, u32[]{:S(2)}, u32[]{:S(2)}) async-start(bf16[32,288,128]{2,1,0:T(8,128)(2,1)} %bitcast_bitcast_fusion), calls=%async_computation | async-start | bytes 4718592 | tf_op jit(solution)/shard_map/all_to_all | solution.py:304
  14.0 1.0 slice-start.1
  14.0 1.4 slice-start.3
  69.7 33.9 %all-to-all-start.1 = ((bf16[32,128,128]{2,1,0:T(8,128)(2,1)}), bf16[32,128,128]{2,1,0:T(8,128)(2,1)S(1)}, u32[]{:S(2)}, u32[]{:S(2)}) async-start(bf16[32,128,128]{2,1,0:T(8,128)(2,1)} %bitcast.1), calls=%async_computation.1 | async-start | bytes 2097152 | tf_op jit(solution)/shard_map/all_to_all | solution.py:304
  103.6 1.0 copy-start
  134.0 39.5 %all-to-all-start.2 = ((bf16[32,96,128]{2,1,0:T(8,128)(2,1)}), bf16[32,96,128]{2,1,0:T(8,128)(2,1)S(1)}, u32[]{:S(2)}, u32[]{:S(2)}) async-start(bf16[32,96,128]{2,1,0:T(8,128)(2,1)} %get-tuple-element.19), calls=%async_computation.2 | async-start | bytes 1572864 | tf_op jit(solution)/shard_map/all_to_all | solution.py:304
  173.5 26.1 %all-to-all-start.3 = ((bf16[32,64,128]{2,1,0:T(8,128)(2,1)}), bf16[32,64,128]{2,1,0:T(8,128)(2,1)S(1)}, u32[]{:S(2)}, u32[]{:S(2)}) async-start(bf16[32,64,128]{2,1,0:T(8,128)(2,1)} %shard_map.79), calls=%async_computation.3 | async-start | bytes 1048576 | tf_op jit(solution)/shard_map/all_to_all | solution.py:304

commit v4 on v3

--- a/solution.py
+++ b/solution.py
@@ -56,7 +56,8 @@
     copies = []
     for g in range(block.shape[0] // group):
         here = pl.ds(g * group, group)
-        copies.append(pltpu.make_async_copy(source.at[here], block.at[here], sems.at[g]))
+        source_rows = pl.ds(0, block.shape[1])
+        copies.append(pltpu.make_async_copy(source.at[here, source_rows, :], block.at[here], sems.at[g]))
         copies[-1].start()
     return copies
 
@@ -94,70 +95,79 @@
             total_ref[index, head] = quick(head, queries[head], key_ref, value_ref)
         return carry
 
-    lax.fori_loop(0, total_ref.shape[0], block, 0)
+    lax.fori_loop(0, total_ref.shape[0], block, 0, unroll=4)
 
 
 def finish_rows(begin, part, query_ref, parts, total_ref, out_ref, fetch_first=None):
     block_rows = SOURCES_AT_ONCE * part
-
-    def block(index, carry):
+    blocks = out_ref.shape[0] // SOURCES_AT_ONCE
+
+    def at(index):
         sources = pl.ds(index * SOURCES_AT_ONCE, SOURCES_AT_ONCE)
-        queries = head_queries(query_ref, sources, begin, part)
 
         def store(totals):
             mixed = jnp.concatenate([t[:DH] / t[DH : DH + 1] for t in totals], axis=0)
             out_ref[sources] = mixed.T.astype(jnp.bfloat16).reshape(SOURCES_AT_ONCE, part, LANES)
 
+        return head_queries(query_ref, sources, begin, part), store
+
+    def quick_block(index, unsafe):
+        queries, store = at(index)
         totals = []
         for head in range(2):
             total = quick(head, queries[head], *parts[0]) if total_ref is None else total_ref[index, head]
             totals.append(total + quick(head, queries[head], *parts[1]))
         store(totals)
-        sums = jnp.concatenate([t[DH : DH + 8] for t in totals], axis=0)
-        safe = jnp.logical_and(sums >= SUM_LOW, sums <= SUM_HIGH)
-        unsafe = jnp.max(jnp.where(safe, 0.0, 1.0)) > 0.0
-
-        @pl.when(unsafe)
-        def _():
-            if fetch_first is not None:
-                fetch_first()
-            pick = lax.broadcasted_iota(jnp.int32, (16, block_rows), 0) == 0
-            pick = jnp.where(pick, 1.0, 0.0).astype(jnp.bfloat16)
-            totals = []
-            for head in range(2):
-
-                def found(key_ref, value_ref, start, head=head):
-                    live = lax.dot_general(
-                        value_ref[head, DH:, pl.ds(start, SLOW_KEYS)],
-                        pick,
-                        CONTRACT_FIRST,
-                        preferred_element_type=jnp.float32,
-                    )
-                    return jnp.where(live > 0.5, scores(key_ref, queries[head], start, SLOW_KEYS), -jnp.inf)
-
-                top = jnp.full((1, block_rows), -jnp.inf, jnp.float32)
-                total = jnp.zeros((DH + 16, block_rows), jnp.float32)
-                for key_ref, value_ref in parts:
-
-                    def first(i, top, key_ref=key_ref, value_ref=value_ref):
-                        start = pl.multiple_of(i * SLOW_KEYS, SLOW_KEYS)
-                        return jnp.maximum(top, jnp.max(found(key_ref, value_ref, start), axis=0, keepdims=True))
-
-                    top = lax.fori_loop(0, key_ref.shape[0] // SLOW_KEYS, first, top)
-                for key_ref, value_ref in parts:
-
-                    def second(i, total, key_ref=key_ref, value_ref=value_ref, head=head, top=top):
-                        start = pl.multiple_of(i * SLOW_KEYS, SLOW_KEYS)
-                        weights = jnp.exp2((found(key_ref, value_ref, start) - top) * EXP2_SCALE)
-                        return total + weigh(value_ref, head, weights, start, SLOW_KEYS)
-
-                    total = lax.fori_loop(0, key_ref.shape[0] // SLOW_KEYS, second, total)
-                totals.append(total)
-            store(totals)
-
+        for total in totals:
+            sums = total[DH : DH + 8]
+            safe = jnp.logical_and(sums >= SUM_LOW, sums <= SUM_HIGH)
+            unsafe = jnp.maximum(unsafe, jnp.where(safe, 0.0, 1.0))
+        return unsafe
+
+    unsafe = lax.fori_loop(0, blocks, quick_block, jnp.zeros((8, block_rows), jnp.float32), unroll=4)
+
+    def careful_block(index, carry):
+        queries, store = at(index)
+        pick = lax.broadcasted_iota(jnp.int32, (16, block_rows), 0) == 0
+        pick = jnp.where(pick, 1.0, 0.0).astype(jnp.bfloat16)
+        totals = []
+        for head in range(2):
+
+            def found(key_ref, value_ref, start, head=head):
+                live = lax.dot_general(
+                    value_ref[head, DH:, pl.ds(start, SLOW_KEYS)],
+                    pick,
+                    CONTRACT_FIRST,
+                    preferred_element_type=jnp.float32,
+                )
+                return jnp.where(live > 0.5, scores(key_ref, queries[head], start, SLOW_KEYS), -jnp.inf)
+
+            top = jnp.full((1, block_rows), -jnp.inf, jnp.float32)
+            total = jnp.zeros((DH + 16, block_rows), jnp.float32)
+            for key_ref, value_ref in parts:
+
+                def first(i, top, key_ref=key_ref, value_ref=value_ref):
+                    start = pl.multiple_of(i * SLOW_KEYS, SLOW_KEYS)
+                    return jnp.maximum(top, jnp.max(found(key_ref, value_ref, start), axis=0, keepdims=True))
+
+                top = lax.fori_loop(0, key_ref.shape[0] // SLOW_KEYS, first, top)
+            for key_ref, value_ref in parts:
+
+                def second(i, total, key_ref=key_ref, value_ref=value_ref, head=head, top=top):
+                    start = pl.multiple_of(i * SLOW_KEYS, SLOW_KEYS)
+                    weights = jnp.exp2((found(key_ref, value_ref, start) - top) * EXP2_SCALE)
+                    return total + weigh(value_ref, head, weights, start, SLOW_KEYS)
+
+                total = lax.fori_loop(0, key_ref.shape[0] // SLOW_KEYS, second, total)
+            totals.append(total)
+        store(totals)
         return carry
 
-    lax.fori_loop(0, out_ref.shape[0] // SOURCES_AT_ONCE, block, 0)
+    @pl.when(jnp.max(unsafe) > 0.0)
+    def _():
+        if fetch_first is not None:
+            fetch_first()
+        lax.fori_loop(0, blocks, careful_block, 0)
 
 
 def begin_kernel(shape, part, length_ref, arrived, total_ref, keys_out, values_out, *scratch):
@@ -271,7 +281,7 @@
         (valid_len, second, first, *early, total),
         work(parts[0], rows_second),
         [
-            pltpu.VMEM(second.shape, second.dtype),
+            pltpu.VMEM((sources, begins[1], LANES), second.dtype),
             query_blocks[0],
             *scratch,
             *early_scratch,

time: 201 us -> 308 us (1.53); the launches traced: 201 us -> 304 us
  Pallas kernels: 84.9 us -> 188 us
    pallas_call x3, Pallas kernels: 84.9 us -> 188 us  [call(): pl.pallas_call(kernel, in_specs=in_specs, out_specs=out_specs, out_shape=...]
  transfers between devices with their start and end apart: 4 -> 4, of which waited for: 3 -> 3; matrix products, arithmetic and copies ran while one was open for 3% -> 2% of each run, Pallas kernels for 28% -> 34%
where the time goes in v4:
time: 308 us; the launch traced here: 304 us
  Pallas kernels  188 us (61%)
  waiting for transfers between devices  74.1 us (24%)
  starting transfers between devices  27.1 us (9%)
  local copies, waits for them, and re-layouts  6.94 us (2%)
  other arithmetic  5.44 us (2%)
    pallas_call x3, Pallas kernels, call(): pl.pallas_call(kernel, in_specs=in_specs, out_specs=out_specs, out_shape=...  188 us
    all_to_all x4, waiting for transfers between devices, exchange(): lax.all_to_all(blocks, 'seq', split_axis=0, concat_axis=0, tiled=True)  74.1 us
    all_to_all x4, starting transfers between devices, exchange(): lax.all_to_all(blocks, 'seq', split_axis=0, concat_axis=0, tiled=True)  27.1 us
  transfers between devices with their start and end apart: 4, of which 3 were waited for; matrix products, arithmetic and copies ran while one was open for 2% of the time, Pallas kernels for 34%

profile of v4, /device:TPU:2, one launch (start us, length us, event | category | flops | bytes accessed | tf_op | source)
XLA Modules:
  0.0 303.8 jit_solution(670849611338574291)
XLA Ops:
  0.6 0.0 slice-start
  0.6 0.0 slice-start.2
  0.7 0.0 copy-start.1
  0.7 1.4 fusion
  2.1 0.0 slice-done
  2.1 0.2 slice-done.2
  2.3 0.0 copy-done.1
  2.4 1.6 bitcast_bitcast_fusion
  4.0 10.0 %all-to-all-start = ((bf16[32,288,128]{2,1,0:T(8,128)(2,1)}), bf16[32,288,128]{2,1,0:T(8,128)(2,1)}, u32[]{:S(2)}, u32[]{:S(2)}) async-start(bf16[32,288,128]{2,1,0:T(8,128)(2,1)} %bitcast_bitcast_fusion), calls=%async_computation | async-start | bytes 4718592 | tf_op jit(solution)/shard_map/all_to_all | solution.py:314
  14.0 0.0 slice-start.1
  14.0 0.0 slice-start.3
  14.0 0.5 copy.18
  14.5 0.4 slice-done.1
  14.9 0.5 copy.16
  15.4 0.0 slice-done.3
  15.4 0.5 copy.17
  15.9 1.9 pad_maximum_fusion
  17.8 2.3 copy.11
  20.1 49.6 %all-to-all-done.arrived.queries = bf16[32,288,128]{2,1,0:T(8,128)(2,1)} async-done(((bf16[32,288,128]{2,1,0:T(8,128)(2,1)}), bf16[32,288,128]{2,1,0:T(8,128)(2,1)}, u32[]{:S(2)}, u32[]{:S(2)}) %all-to-all-start) | async-done | bytes 2359328 | tf_op jit(solution)/shard_map/all_to_all | solution.py:314
  69.7 5.0 %all-to-all-start.1 = ((bf16[32,128,128]{2,1,0:T(8,128)(2,1)}), bf16[32,128,128]{2,1,0:T(8,128)(2,1)S(1)}, u32[]{:S(2)}, u32[]{:S(2)}) async-start(bf16[32,128,128]{2,1,0:T(8,128)(2,1)} %bitcast.1), calls=%async_computation.1 | async-start | bytes 2097152 | tf_op jit(solution)/shard_map/all_to_all | solution.py:314
  76.0 20.4 %shard_map.77 = (f32[4,2,80,768]{3,2,1,0:T(8,128)}, bf16[3072,128]{1,0:T(8,128)(2,1)}, bf16[2,80,3072]{2,1,0:T(8,128)(2,1)}) custom-call(s32[1]{0:T(128)S(6)} %copy.27.length_ref, bf16[32,288,128]{2,1,0:T(8,128)(2,1)} %all-to-all-done.arrived.queries), custom_call_target="tpu_custom_call" | custom-call | flops 19327352832 | bytes 8388608 | tf_op jit(solution)/shard_map/pallas_call | solution.py:234
  96.4 7.3 %all-to-all-done.1.arrived.queries = bf16[32,128,128]{2,1,0:T(8,128)(2,1)S(1)} async-done(((bf16[32,128,128]{2,1,0:T(8,128)(2,1)}), bf16[32,128,128]{2,1,0:T(8,128)(2,1)S(1)}, u32[]{:S(2)}, u32[]{:S(2)}) %all-to-all-start.1) | async-done | bytes 1048608 | tf_op jit(solution)/shard_map/all_to_all | solution.py:314
  103.6 0.0 copy-start
  103.6 1.0 copy-done
  104.6 83.8 %shard_map.78 = (bf16[32,96,128]{2,1,0:T(8,128)(2,1)}, bf16[1024,128]{1,0:T(8,128)(2,1)}, bf16[2,80,1024]{2,1,0:T(8,128)(2,1)}) custom-call(s32[1]{0:T(128)S(6)} %copy.27.length_ref, bf16[32,128,128]{2,1,0:T(8,128)(2,1)} %copy-done, bf16[32,288,128]{2,1,0:T(8,128)(2,1)} %all-to-all-done.arrived.queries, ...), custom_call_target="tpu_custom_call" | custom-call | flops 6442450944 | bytes 8388608 | tf_op jit(solution)/shard_map/pallas_call | solution.py:234
  188.4 3.9 %all-to-all-start.2 = ((bf16[32,96,128]{2,1,0:T(8,128)(2,1)}), bf16[32,96,128]{2,1,0:T(8,128)(2,1)S(1)}, u32[]{:S(2)}, u32[]{:S(2)}) async-start(bf16[32,96,128]{2,1,0:T(8,128)(2,1)} %get-tuple-element.19), calls=%async_computation.2 | async-start | bytes 1572864 | tf_op jit(solution)/shard_map/all_to_all | solution.py:314
  192.4 83.7 %shard_map.79 = bf16[32,64,128]{2,1,0:T(8,128)(2,1)} custom-call(bf16[32,128,128]{2,1,0:T(8,128)(2,1)} %copy-done, bf16[3072,128]{1,0:T(8,128)(2,1)} %get-tuple-element.14.refs_0_.early_keys, bf16[2,80,3072]{2,1,0:T(8,128)(2,1)} %get-tuple-element.15.refs_1_.early_values, bf16[1024,128]{1,0:T(8,128)(2,1)} %get-tuple-element.17.keys, ...), custom_call_target="tpu_custom_call" | custom-call | flops 17179869184 | bytes 8388608 | tf_op jit(solution)/shard_map/pallas_call | solution.py:234
  276.1 0.0 all-to-all-done.2
  276.1 8.3 %all-to-all-start.3 = ((bf16[32,64,128]{2,1,0:T(8,128)(2,1)}), bf16[32,64,128]{2,1,0:T(8,128)(2,1)S(1)}, u32[]{:S(2)}, u32[]{:S(2)}) async-start(bf16[32,64,128]{2,1,0:T(8,128)(2,1)} %shard_map.79), calls=%async_computation.3 | async-start | bytes 1048576 | tf_op jit(solution)/shard_map/all_to_all | solution.py:314
  284.4 0.8 bitcast_select_fusion
  285.2 17.2 %all-to-all-done.3 = bf16[32,64,128]{2,1,0:T(8,128)(2,1)S(1)} async-done(((bf16[32,64,128]{2,1,0:T(8,128)(2,1)}), bf16[32,64,128]{2,1,0:T(8,128)(2,1)S(1)}, u32[]{:S(2)}, u32[]{:S(2)}) %all-to-all-start.3) | async-done | bytes 524320 | tf_op jit(solution)/shard_map/all_to_all | solution.py:314
  302.4 0.1 copy_bitcast_fusion
  302.5 1.1 pad_maximum_fusion.1
  (2 shorter events, 0.0 us)
Async XLA Ops:
  0.6 1.5 slice-start
  0.6 1.7 slice-start.2
  0.7 1.7 copy-start.1
  4.0 65.7 %all-to-all-start = ((bf16[32,288,128]{2,1,0:T(8,128)(2,1)}), bf16[32,288,128]{2,1,0:T(8,128)(2,1)}, u32[]{:S(2)}, u32[]{:S(2)}) async-start(bf16[32,288,128]{2,1,0:T(8,128)(2,1)} %bitcast_bitcast_fusion), calls=%async_computation | async-start | bytes 4718592 | tf_op jit(solution)/shard_map/all_to_all | solution.py:314
  14.0 1.0 slice-start.1
  14.0 1.4 slice-start.3
  69.7 33.9 %all-to-all-start.1 = ((bf16[32,128,128]{2,1,0:T(8,128)(2,1)}), bf16[32,128,128]{2,1,0:T(8,128)(2,1)S(1)}, u32[]{:S(2)}, u32[]{:S(2)}) async-start(bf16[32,128,128]{2,1,0:T(8,128)(2,1)} %bitcast.1), calls=%async_computation.1 | async-start | bytes 2097152 | tf_op jit(solution)/shard_map/all_to_all | solution.py:314
  103.6 1.0 copy-start
  188.4 87.6 %all-to-all-start.2 = ((bf16[32,96,128]{2,1,0:T(8,128)(2,1)}), bf16[32,96,128]{2,1,0:T(8,128)(2,1)S(1)}, u32[]{:S(2)}, u32[]{:S(2)}) async-start(bf16[32,96,128]{2,1,0:T(8,128)(2,1)} %get-tuple-element.19), calls=%async_computation.2 | async-start | bytes 1572864 | tf_op jit(solution)/shard_map/all_to_all | solution.py:314
  276.1 26.3 %all-to-all-start.3 = ((bf16[32,64,128]{2,1,0:T(8,128)(2,1)}), bf16[32,64,128]{2,1,0:T(8,128)(2,1)S(1)}, u32[]{:S(2)}, u32[]{:S(2)}) async-start(bf16[32,64,128]{2,1,0:T(8,128)(2,1)} %shard_map.79), calls=%async_computation.3 | async-start | bytes 1048576 | tf_op jit(solution)/shard_map/all_to_all | solution.py:314
